TPU v7x, 512 devices: a whole 4x4x16 slice. The times are simulated.
512 devices in a mesh: grp: 16 (over x, y_lo, core), loop: 32 (over y_hi, z).
Axes of the slice: x: 4, y: 4 (y_hi: 2, y_lo: 2; y = y_hi * 2 + y_lo), z: 16, core: 2. Of those that a mesh axis runs over, the one named last changes fastest.
Arguments:
- vision_tower_output: bfloat16 [32768, 1536], P(('grp', 'loop')), may hold values from -0.1796875 to 0.1796875
- language_tower_output: bfloat16 [32768, 1536], P(('grp', 'loop')), may hold values from -0.1796875 to 0.1796875
- sharpness_factor: float32 [1], replicated, may hold values from 4 to 16
- shift_added: float32 [1], replicated, may hold values from -3 to -1
Outputs:
- image_gradient: float32 [32768, 1536], P(('grp', 'loop'))
- grad_texts: float32 [32768, 1536], P(('grp', 'loop'))
All inputs are finite; a program needn't handle non-finite values.
Results may differ from a plain program's by a relative error of at most 0.023.
Values may be sent and summed in bfloat16 or wider, within the bound.
A program may use at most 128 MiB of HBM per device.

v0:
```python
import jax
import jax.numpy as jnp
from jax import lax
from jax.sharding import PartitionSpec as P

HOPS = 4


def from_behind(block, axis, distance):
    devices = range(lax.axis_size(axis))
    route = [((i - distance) % len(devices), i) for i in devices]
    return lax.ppermute(block, axis, route)


def normalize_each_entry_line(values):
    wide = values.astype(jnp.float32)
    inverse = lax.rsqrt(jnp.sum(wide * wide, axis=-1, keepdims=True) + 1e-06)
    return (wide * inverse, inverse)


def pair_coef(picture_rows, txt_rows, similarity_multiplier, group_offset, positive):
    score = (
        lax.dot_general(
            picture_rows, txt_rows, (((1,), (1,)), ((), ())), preferred_element_type=jnp.float32
        )
        * similarity_multiplier
        + group_offset
    )
    sign = jnp.where(positive, 1.0, -1.0).astype(jnp.float32)
    return (-sign * jax.nn.sigmoid(-sign * score) * similarity_multiplier).astype(jnp.bfloat16)


def back_norm(unit, inverse, grad):
    return (grad - unit * jnp.sum(unit * grad, axis=-1, keepdims=True)) * inverse


def per_device(vision_tower_output, language_tower_output, sharpness_factor, shift_added):
    similarity_multiplier = sharpness_factor[0]
    group_offset = shift_added[0]
    rows = vision_tower_output.shape[0]
    unit_img, inv_img = normalize_each_entry_line(vision_tower_output)
    unit_txt, reciprocal_textual_norm = normalize_each_entry_line(language_tower_output)
    visual_embedding_vectors = unit_img.astype(jnp.bfloat16)
    emb_txt = unit_txt.astype(jnp.bfloat16)
    block = lax.all_gather(emb_txt, "grp", axis=0, tiled=True)
    member = lax.axis_index("grp")
    columns = lax.broadcasted_iota(jnp.int32, (rows, block.shape[0]), 1)
    row_ids = lax.broadcasted_iota(jnp.int32, (rows, block.shape[0]), 0)
    positive = columns == member * rows + row_ids
    first = pair_coef(
        visual_embedding_vectors, block, similarity_multiplier, group_offset, positive
    )
    grad_emb = jnp.dot(first, block, preferred_element_type=jnp.float32)
    factors = [(first, visual_embedding_vectors)]
    for step in range(1, HOPS + 1):
        visitor = from_behind(visual_embedding_vectors, "loop", -step)
        coef = pair_coef(visitor, block, similarity_multiplier, group_offset, False)
        term = jnp.dot(coef, block, preferred_element_type=jnp.float32)
        grad_emb = grad_emb + from_behind(term.astype(jnp.bfloat16), "loop", step).astype(
            term.dtype
        )
        factors.append((coef, visitor))
    total = jnp.zeros((rows * lax.axis_size("grp"), emb_txt.shape[1]), jnp.float32)
    for coef, picture_rows in factors:
        total = total + lax.dot_general(
            coef, picture_rows, (((0,), (0,)), ((), ())), preferred_element_type=jnp.float32
        )
    grad_txt_emb = lax.psum_scatter(
        total.astype(jnp.bfloat16), "grp", scatter_dimension=0, tiled=True
    ).astype(jnp.float32)
    return (
        back_norm(unit_img, inv_img, grad_emb),
        back_norm(unit_txt, reciprocal_textual_norm, grad_txt_emb),
    )


def solution(mesh):
    in_specs = (P(("grp", "loop"), None), P(("grp", "loop"), None), P(), P())
    out_specs = (P(("grp", "loop"), None), P(("grp", "loop"), None))
    return jax.shard_map(
        per_device, mesh=mesh, in_specs=in_specs, out_specs=out_specs, check_vma=False
    )
```

profile of v0, /device:TPU:16, one launch (start us, length us, event | category | flops | bytes accessed | tf_op | source)
XLA Modules:
  0.0 185.3 jit_solution(16444685629721222830)
XLA Ops:
  12.9 12.5 %collective-permute-start.6 = (bf16[64,1536]{1,0:T(8,128)(2,1)}, bf16[64,1536]{1,0:T(8,128)(2,1)}, u32[]{:S(2)}, u32[]{:S(2)}) collective-permute-start(bf16[64,1536]{1,0:T(8,128)(2,1)} %fusion.41), channel_id=1, source_target_pairs={{4,0},{5,1},{6,2},{7,3},{8,4},{9,5},{10,6},{11,7},{12,8},{13,9},{1... | collective-permute-start | bytes 589832 | tf_op jit(solution)/shard_map/ppermute | solution.py:12
  25.4 5.0 %collective-permute-start.4 = (bf16[64,1536]{1,0:T(8,128)(2,1)}, bf16[64,1536]{1,0:T(8,128)(2,1)}, u32[]{:S(2)}, u32[]{:S(2)}) collective-permute-start(bf16[64,1536]{1,0:T(8,128)(2,1)} %fusion.41), channel_id=1, source_target_pairs={{3,0},{4,1},{5,2},{6,3},{7,4},{8,5},{9,6},{10,7},{11,8},{12,9},{13... | collective-permute-start | bytes 589832 | tf_op jit(solution)/shard_map/ppermute | solution.py:12
  30.4 2.5 %collective-permute-start.2 = (bf16[64,1536]{1,0:T(8,128)(2,1)}, bf16[64,1536]{1,0:T(8,128)(2,1)}, u32[]{:S(2)}, u32[]{:S(2)}) collective-permute-start(bf16[64,1536]{1,0:T(8,128)(2,1)} %fusion.41), channel_id=1, source_target_pairs={{2,0},{3,1},{4,2},{5,3},{6,4},{7,5},{8,6},{9,7},{10,8},{11,9},{12,... | collective-permute-start | bytes 589832 | tf_op jit(solution)/shard_map/ppermute | solution.py:12
  32.9 2.4 %collective-permute-start = (bf16[64,1536]{1,0:T(8,128)(2,1)}, bf16[64,1536]{1,0:T(8,128)(2,1)S(1)}, u32[]{:S(2)}, u32[]{:S(2)}) collective-permute-start(bf16[64,1536]{1,0:T(8,128)(2,1)} %fusion.41), channel_id=1, source_target_pairs={{1,0},{2,1},{3,2},{4,3},{5,4},{6,5},{7,6},{8,7},{9,8},{10,9},{11,1... | collective-permute-start | bytes 589832 | tf_op jit(solution)/shard_map/ppermute | solution.py:12
  36.6 21.6 %all-gather.2.cloned.1.call-done = bf16[1024,1536]{1,0:T(8,128)(2,1)} async-done(((bf16[64,1536]{1,0:T(8,128)(2,1)}), bf16[1024,1536]{1,0:T(8,128)(2,1)}) %all-gather.2.cloned.1.call-update) | async-done | bytes 3145744 | tf_op jit(solution)/shard_map/all_gather | solution.py:45
  58.1 3.1 %fusion.32 = bf16[64,1024]{1,0:T(8,128)(2,1)S(1)} fusion(bf16[64,1536]{1,0:T(8,128)(2,1)} %fusion.41, bf16[1024,1536]{1,0:T(8,128)(2,1)} %all-gather.2.cloned.1.call-done, f32[]{:T(128)} %bitcast.37, f32[]{:T(128)} %bitcast.36, s32[64]{0:T(128)S(1)} %iota_add_fusion), kind=kOutput, calls=%fused_computation.42 | convolution fusion | flops 202113024 | bytes 3473672 | tf_op jit(solution)/shard_map/dot_general | solution.py:23
  61.2 2.1 %fusion.49 = f32[1024,1536]{1,0:T(8,128)S(1)} fusion(bf16[64,1024]{1,0:T(8,128)(2,1)S(1)} %fusion.32, bf16[64,1536]{1,0:T(8,128)(2,1)} %fusion.41), kind=kOutput, calls=%fused_computation.70 | convolution fusion | flops 201326592 | bytes 6619136 | tf_op jit(solution)/shard_map/dot_general | solution.py:65
  63.3 4.5 %collective-permute-done = bf16[64,1536]{1,0:T(8,128)(2,1)S(1)} collective-permute-done((bf16[64,1536]{1,0:T(8,128)(2,1)}, bf16[64,1536]{1,0:T(8,128)(2,1)S(1)}, u32[]{:S(2)}, u32[]{:S(2)}) %collective-permute-start) | collective-permute-done | bytes 196640 | tf_op jit(solution)/shard_map/ppermute | solution.py:12
  68.5 2.1 %fusion.36 = bf16[64,1024]{1,0:T(8,128)(2,1)S(1)} fusion(bf16[64,1536]{1,0:T(8,128)(2,1)} %copy-done.7, bf16[1024,1536]{1,0:T(8,128)(2,1)S(1)} %copy-done, f32[]{:T(128)} %bitcast.41, f32[]{:T(128)} %bitcast.34), kind=kOutput, calls=%fused_computation.46 | convolution fusion | flops 201785344 | bytes 3473416 | tf_op jit(solution)/shard_map/dot_general | solution.py:23
  71.6 2.0 %fusion.35 = bf16[64,1024]{1,0:T(8,128)(2,1)S(1)} fusion(bf16[64,1536]{1,0:T(8,128)(2,1)} %collective-permute-done.2, bf16[1024,1536]{1,0:T(8,128)(2,1)S(1)} %copy-done, f32[]{:T(128)} %bitcast.40, f32[]{:T(128)} %bitcast.35), kind=kOutput, calls=%fused_computation.45 | convolution fusion | flops 201785344 | bytes 3473416 | tf_op jit(solution)/shard_map/dot_general | solution.py:23
  73.6 4.6 %fusion.51 = f32[1024,1536]{1,0:T(8,128)} fusion(bf16[64,1024]{1,0:T(8,128)(2,1)S(1)} %fusion.35, bf16[64,1536]{1,0:T(8,128)(2,1)} %collective-permute-done.2), kind=kOutput, calls=%fused_computation.72 | convolution fusion | flops 201326592 | bytes 6619136 | tf_op jit(solution)/shard_map/dot_general | solution.py:65
  78.3 2.0 %fusion.34 = bf16[64,1024]{1,0:T(8,128)(2,1)S(1)} fusion(bf16[64,1536]{1,0:T(8,128)(2,1)} %collective-permute-done.4, bf16[1024,1536]{1,0:T(8,128)(2,1)S(1)} %copy-done, f32[]{:T(128)} %bitcast.39, f32[]{:T(128)} %bitcast.33), kind=kOutput, calls=%fused_computation.44 | convolution fusion | flops 201785344 | bytes 3473416 | tf_op jit(solution)/shard_map/dot_general | solution.py:23
  80.3 4.6 %fusion.52 = f32[1024,1536]{1,0:T(8,128)} fusion(bf16[64,1024]{1,0:T(8,128)(2,1)S(1)} %fusion.34, bf16[64,1536]{1,0:T(8,128)(2,1)} %collective-permute-done.4), kind=kOutput, calls=%fused_computation.73 | convolution fusion | flops 201326592 | bytes 6619136 | tf_op jit(solution)/shard_map/dot_general | solution.py:65
  84.9 2.0 %fusion.33 = bf16[64,1024]{1,0:T(8,128)(2,1)S(1)} fusion(bf16[64,1536]{1,0:T(8,128)(2,1)} %collective-permute-done.6, bf16[1024,1536]{1,0:T(8,128)(2,1)S(1)} %copy-done, f32[]{:T(128)} %bitcast.38, f32[]{:T(128)} %bitcast.32), kind=kOutput, calls=%fused_computation.43 | convolution fusion | flops 201785344 | bytes 3473416 | tf_op jit(solution)/shard_map/dot_general | solution.py:23
  87.0 8.3 %add_convert_fusion = bf16[1024,1536]{1,0:T(8,128)(2,1)} fusion(f32[1024,1536]{1,0:T(8,128)} %fusion.52, f32[1024,1536]{1,0:T(8,128)} %fusion.51, f32[1024,1536]{1,0:T(8,128)S(1)} %fusion.49, f32[1024,1536]{1,0:T(8,128)S(1)} %fusion.50, bf16[64,1024]{1,0:T(8,128)(2,1)S(1)} %fusion.33, bf16[64,1536]{1,0:T(8,128)(2,1)} %collective-permute-done.6), kind=kOutput, calls=%fused_computation | convolution fusion | flops 209190912 | bytes 28639232 | tf_op jit(solution)/shard_map/dot_general | solution.py:65
  96.0 3.2 %collective-permute-start.7 = (bf16[64,1536]{1,0:T(8,128)(2,1)S(1)}, bf16[64,1536]{1,0:T(8,128)(2,1)S(1)}, u32[]{:S(2)}, u32[]{:S(2)}) collective-permute-start(bf16[64,1536]{1,0:T(8,128)(2,1)S(1)} %convolution_convert_fusion), channel_id=1, source_target_pairs={{28,0},{29,1},{30,2},{31,3},{0,4},{1,5},{2,6},{3,7},{4,8},{5,9},{6... | collective-permute-start | bytes 589832 | tf_op jit(solution)/shard_map/ppermute | solution.py:12
  99.9 5.7 %collective-permute-start.5 = (bf16[64,1536]{1,0:T(8,128)(2,1)S(1)}, bf16[64,1536]{1,0:T(8,128)(2,1)S(1)}, u32[]{:S(2)}, u32[]{:S(2)}) collective-permute-start(bf16[64,1536]{1,0:T(8,128)(2,1)S(1)} %convolution_convert_fusion.1), channel_id=1, source_target_pairs={{29,0},{30,1},{31,2},{0,3},{1,4},{2,5},{3,6},{4,7},{5,8},{6,9},{7,... | collective-permute-start | bytes 589832 | tf_op jit(solution)/shard_map/ppermute | solution.py:12
  106.2 4.6 %collective-permute-start.3 = (bf16[64,1536]{1,0:T(8,128)(2,1)S(1)}, bf16[64,1536]{1,0:T(8,128)(2,1)S(1)}, u32[]{:S(2)}, u32[]{:S(2)}) collective-permute-start(bf16[64,1536]{1,0:T(8,128)(2,1)S(1)} %convolution_convert_fusion.2), channel_id=1, source_target_pairs={{30,0},{31,1},{0,2},{1,3},{2,4},{3,5},{4,6},{5,7},{6,8},{7,9},{8,1... | collective-permute-start | bytes 589832 | tf_op jit(solution)/shard_map/ppermute | solution.py:12
  111.6 3.3 %collective-permute-start.1 = (bf16[64,1536]{1,0:T(8,128)(2,1)S(1)}, bf16[64,1536]{1,0:T(8,128)(2,1)S(1)}, u32[]{:S(2)}, u32[]{:S(2)}) collective-permute-start(bf16[64,1536]{1,0:T(8,128)(2,1)S(1)} %convolution_convert_fusion.3), channel_id=1, source_target_pairs={{31,0},{0,1},{1,2},{2,3},{3,4},{4,5},{5,6},{6,7},{7,8},{8,9},{9,10... | collective-permute-start | bytes 589832 | tf_op jit(solution)/shard_map/ppermute | solution.py:12
  114.9 23.0 %collective-permute-done.5 = bf16[64,1536]{1,0:T(8,128)(2,1)S(1)} collective-permute-done((bf16[64,1536]{1,0:T(8,128)(2,1)S(1)}, bf16[64,1536]{1,0:T(8,128)(2,1)S(1)}, u32[]{:S(2)}, u32[]{:S(2)}) %collective-permute-start.5) | collective-permute-done | bytes 196640 | tf_op jit(solution)/shard_map/ppermute | solution.py:12
  137.8 3.7 %collective-permute-done.3 = bf16[64,1536]{1,0:T(8,128)(2,1)S(1)} collective-permute-done((bf16[64,1536]{1,0:T(8,128)(2,1)S(1)}, bf16[64,1536]{1,0:T(8,128)(2,1)S(1)}, u32[]{:S(2)}, u32[]{:S(2)}) %collective-permute-start.3) | collective-permute-done | bytes 196640 | tf_op jit(solution)/shard_map/ppermute | solution.py:12
  141.6 6.4 %collective-permute-done.1 = bf16[64,1536]{1,0:T(8,128)(2,1)S(1)} collective-permute-done((bf16[64,1536]{1,0:T(8,128)(2,1)S(1)}, bf16[64,1536]{1,0:T(8,128)(2,1)S(1)}, u32[]{:S(2)}, u32[]{:S(2)}) %collective-permute-start.1) | collective-permute-done | bytes 196640 | tf_op jit(solution)/shard_map/ppermute | solution.py:12
  149.8 25.6 %reduce-scatter.2.cloned.1.call-done = bf16[64,1536]{1,0:T(8,128)(2,1)} async-done(((bf16[1024,1536]{1,0:T(8,128)(2,1)}), bf16[64,1536]{1,0:T(8,128)(2,1)}) %reduce-scatter.2.cloned.1.call-update) | async-done | bytes 196624 | tf_op jit(solution)/shard_map/reduce_scatter | solution.py:68
  176.6 1.8 fusion.48
  (41 shorter events, 13.0 us)
Async XLA Ops:
  7.2 51.0 %all-gather.2.cloned.1.call-start = ((), (), s32[]{:S(2)}) async-start(), calls=%async_computation.1 | async-start | bytes 3342336 | tf_op jit(solution)/shard_map/all_gather | solution.py:45
  10.0 165.4 %reduce-scatter.2.cloned.1.call-start = ((), (), s32[]{:S(2)}) async-start(), calls=%async_computation.2 | async-start | bytes 3342336 | tf_op jit(solution)/shard_map/reduce_scatter | solution.py:68
  12.9 72.1 %collective-permute-start.6 = (bf16[64,1536]{1,0:T(8,128)(2,1)}, bf16[64,1536]{1,0:T(8,128)(2,1)}, u32[]{:S(2)}, u32[]{:S(2)}) collective-permute-start(bf16[64,1536]{1,0:T(8,128)(2,1)} %fusion.41), channel_id=1, source_target_pairs={{4,0},{5,1},{6,2},{7,3},{8,4},{9,5},{10,6},{11,7},{12,8},{13,9},{1... | collective-permute-start | bytes 589832 | tf_op jit(solution)/shard_map/ppermute | solution.py:12
  25.4 52.9 %collective-permute-start.4 = (bf16[64,1536]{1,0:T(8,128)(2,1)}, bf16[64,1536]{1,0:T(8,128)(2,1)}, u32[]{:S(2)}, u32[]{:S(2)}) collective-permute-start(bf16[64,1536]{1,0:T(8,128)(2,1)} %fusion.41), channel_id=1, source_target_pairs={{3,0},{4,1},{5,2},{6,3},{7,4},{8,5},{9,6},{10,7},{11,8},{12,9},{13... | collective-permute-start | bytes 589832 | tf_op jit(solution)/shard_map/ppermute | solution.py:12
  30.4 41.2 %collective-permute-start.2 = (bf16[64,1536]{1,0:T(8,128)(2,1)}, bf16[64,1536]{1,0:T(8,128)(2,1)}, u32[]{:S(2)}, u32[]{:S(2)}) collective-permute-start(bf16[64,1536]{1,0:T(8,128)(2,1)} %fusion.41), channel_id=1, source_target_pairs={{2,0},{3,1},{4,2},{5,3},{6,4},{7,5},{8,6},{9,7},{10,8},{11,9},{12,... | collective-permute-start | bytes 589832 | tf_op jit(solution)/shard_map/ppermute | solution.py:12
  32.9 34.9 %collective-permute-start = (bf16[64,1536]{1,0:T(8,128)(2,1)}, bf16[64,1536]{1,0:T(8,128)(2,1)S(1)}, u32[]{:S(2)}, u32[]{:S(2)}) collective-permute-start(bf16[64,1536]{1,0:T(8,128)(2,1)} %fusion.41), channel_id=1, source_target_pairs={{1,0},{2,1},{3,2},{4,3},{5,4},{6,5},{7,6},{8,7},{9,8},{10,9},{11,1... | collective-permute-start | bytes 589832 | tf_op jit(solution)/shard_map/ppermute | solution.py:12
  61.2 7.2 %copy-start = (bf16[1024,1536]{1,0:T(8,128)(2,1)S(1)}, bf16[1024,1536]{1,0:T(8,128)(2,1)}, u32[]{:S(2)}) copy-start(bf16[1024,1536]{1,0:T(8,128)(2,1)} %all-gather.2.cloned.1.call-done) | copy-start | bytes 9437188
  67.8 0.7 copy-start.7
  68.5 2.1 %copy-start.8 = (bf16[64,1536]{1,0:T(8,128)(2,1)S(1)}, bf16[64,1536]{1,0:T(8,128)(2,1)}, u32[]{:S(2)}) copy-start(bf16[64,1536]{1,0:T(8,128)(2,1)} %copy-done.7) | copy-start | bytes 589828
  73.6 4.7 %copy-start.3 = (bf16[64,1024]{1,0:T(8,128)(2,1)}, bf16[64,1024]{1,0:T(8,128)(2,1)S(1)}, u32[]{:S(2)}) copy-start(bf16[64,1024]{1,0:T(8,128)(2,1)S(1)} %fusion.35) | copy-start | bytes 393220
  80.3 4.6 %copy-start.5 = (bf16[64,1024]{1,0:T(8,128)(2,1)}, bf16[64,1024]{1,0:T(8,128)(2,1)S(1)}, u32[]{:S(2)}) copy-start(bf16[64,1024]{1,0:T(8,128)(2,1)S(1)} %fusion.34) | copy-start | bytes 393220
  95.3 3.9 %copy-start.6 = (bf16[64,1024]{1,0:T(8,128)(2,1)S(1)}, bf16[64,1024]{1,0:T(8,128)(2,1)}, u32[]{:S(2)}) copy-start(bf16[64,1024]{1,0:T(8,128)(2,1)} %copy-done.5) | copy-start | bytes 393220
  95.3 10.3 %copy-start.4 = (bf16[64,1024]{1,0:T(8,128)(2,1)S(1)}, bf16[64,1024]{1,0:T(8,128)(2,1)}, u32[]{:S(2)}) copy-start(bf16[64,1024]{1,0:T(8,128)(2,1)} %copy-done.3) | copy-start | bytes 393220
  96.0 18.9 %collective-permute-start.7 = (bf16[64,1536]{1,0:T(8,128)(2,1)S(1)}, bf16[64,1536]{1,0:T(8,128)(2,1)S(1)}, u32[]{:S(2)}, u32[]{:S(2)}) collective-permute-start(bf16[64,1536]{1,0:T(8,128)(2,1)S(1)} %convolution_convert_fusion), channel_id=1, source_target_pairs={{28,0},{29,1},{30,2},{31,3},{0,4},{1,5},{2,6},{3,7},{4,8},{5,9},{6... | collective-permute-start | bytes 589832 | tf_op jit(solution)/shard_map/ppermute | solution.py:12
  99.8 48.1 %copy-start.1 = (bf16[64,1536]{1,0:T(8,128)(2,1)S(1)}, bf16[64,1536]{1,0:T(8,128)(2,1)}, u32[]{:S(2)}) copy-start(bf16[64,1536]{1,0:T(8,128)(2,1)} %param.4) | copy-start | bytes 589828
  99.9 38.0 %collective-permute-start.5 = (bf16[64,1536]{1,0:T(8,128)(2,1)S(1)}, bf16[64,1536]{1,0:T(8,128)(2,1)S(1)}, u32[]{:S(2)}, u32[]{:S(2)}) collective-permute-start(bf16[64,1536]{1,0:T(8,128)(2,1)S(1)} %convolution_convert_fusion.1), channel_id=1, source_target_pairs={{29,0},{30,1},{31,2},{0,3},{1,4},{2,5},{3,6},{4,7},{5,8},{6,9},{7,... | collective-permute-start | bytes 589832 | tf_op jit(solution)/shard_map/ppermute | solution.py:12
  106.2 35.3 %collective-permute-start.3 = (bf16[64,1536]{1,0:T(8,128)(2,1)S(1)}, bf16[64,1536]{1,0:T(8,128)(2,1)S(1)}, u32[]{:S(2)}, u32[]{:S(2)}) collective-permute-start(bf16[64,1536]{1,0:T(8,128)(2,1)S(1)} %convolution_convert_fusion.2), channel_id=1, source_target_pairs={{30,0},{31,1},{0,2},{1,3},{2,4},{3,5},{4,6},{5,7},{6,8},{7,9},{8,1... | collective-permute-start | bytes 589832 | tf_op jit(solution)/shard_map/ppermute | solution.py:12
  111.5 63.9 %copy-start.2 = (bf16[64,1536]{1,0:T(8,128)(2,1)S(1)}, bf16[64,1536]{1,0:T(8,128)(2,1)}, u32[]{:S(2)}) copy-start(bf16[64,1536]{1,0:T(8,128)(2,1)} %param.5) | copy-start | bytes 589828
  111.6 36.4 %collective-permute-start.1 = (bf16[64,1536]{1,0:T(8,128)(2,1)S(1)}, bf16[64,1536]{1,0:T(8,128)(2,1)S(1)}, u32[]{:S(2)}, u32[]{:S(2)}) collective-permute-start(bf16[64,1536]{1,0:T(8,128)(2,1)S(1)} %convolution_convert_fusion.3), channel_id=1, source_target_pairs={{31,0},{0,1},{1,2},{2,3},{3,4},{4,5},{5,6},{6,7},{7,8},{8,9},{9,10... | collective-permute-start | bytes 589832 | tf_op jit(solution)/shard_map/ppermute | solution.py:12
Sparse Core Ops, SparseCore 0:
  10.7 47.3 all-gather.1
  95.4 79.9 reduce-scatter.1
where the time goes:
time: 186 us; the launch traced here: 185 us
  waiting for transfers between devices  84.8 us (46%)
  starting transfers between devices  39.2 us (21%)
  matrix products  35.3 us (19%)
  between operations  15.6 us (8%)
  other arithmetic  9.53 us (5%)
    ppermute x8, starting transfers between devices, from_behind(): return lax.ppermute(block, axis, route)  39.2 us
    ppermute x8, waiting for transfers between devices, from_behind(): return lax.ppermute(block, axis, route)  37.6 us
    reduce_scatter x1, waiting for transfers between devices, per_device(): lax.psum_scatter(total.astype(jnp.bfloat16), 'grp', scatter_dimension=0,...  25.6 us
    all_gather x1, waiting for transfers between devices, per_device(): block = lax.all_gather(emb_txt, 'grp', axis=0, tiled=True)  21.6 us
    dot_general x5, matrix products, per_device(): lax.dot_general(coef, picture_rows, (((0,), (0,)), ((), ())), preferred_e...  20.6 us
    dot_general x5, matrix products, pair_coef(): lax.dot_general(picture_rows, txt_rows, (((1,), (1,)), ((), ())), preferr...  11.3 us
  transfers between devices with their start and end apart: 10, of which 6 were waited for; matrix products, arithmetic and copies ran while one was open for 16% of the time, Pallas kernels for 0%

commit v1 on v0

v1 whole, which is shorter than its diff:
```python
import functools

import jax
import jax.numpy as jnp
from jax import lax
from jax.experimental import pallas as pl
from jax.experimental.pallas import tpu as pltpu
from jax.sharding import PartitionSpec as P

HOPS = 4
ROWS = 64
HALF = 32
WIDE = 1536
XS = 4
MESH = pl.DeviceIdType.MESH
F32 = jnp.float32
BF16 = jnp.bfloat16


def half(c):
    return pl.ds(c * HALF, HALF)


def inverse_norm(ref):
    wide = ref[...].astype(F32)
    return lax.rsqrt(jnp.sum(wide * wide, axis=-1, keepdims=True) + 1e-06)


def back_norm(raw_ref, inverse, grad):
    unit = raw_ref[...].astype(F32) * inverse
    return (grad - unit * jnp.sum(unit * grad, axis=-1, keepdims=True)) * inverse


def kernel(
    loops,
    factor_ref,
    shift_ref,
    img_ref,
    txt_ref,
    img_out,
    txt_out,
    imgs,
    txts,
    coefs,
    grads,
    text_sum,
    other_out,
    other_in,
    chain_out,
    chain_in,
    part_out,
    first_a,
    first_b,
    second,
    row_out,
    row_in,
    send_sem,
    recv_sem,
):
    g = lax.axis_index("grp")
    q = lax.axis_index("loop")
    x = g // 4
    y = (g // 2) % 2
    core = g % 2

    def member(xx, yy, cc):
        return {"grp": xx * 4 + yy * 2 + cc, "loop": q}

    twin = member(x, y, 1 - core)
    across = member(x, 1 - y, core)
    right = member((x + 1) % XS, y, core)
    left = member((x + XS - 1) % XS, y, core)
    below = {"grp": g, "loop": (q + loops - 1) % loops}
    above = {"grp": g, "loop": (q + 1) % loops}

    barrier = pltpu.get_barrier_semaphore()
    peers = (twin, across, right, left, below, above)
    for peer in peers:
        pl.semaphore_signal(barrier, inc=1, device_id=peer, device_id_type=MESH)

    copies = []

    def link(src, dst, device):
        i = len(copies)
        copy = pltpu.make_async_remote_copy(
            src_ref=src,
            dst_ref=dst,
            send_sem=send_sem.at[i],
            recv_sem=recv_sem.at[i],
            device_id=device,
            device_id_type=MESH,
        )
        copies.append(copy)
        return copy

    down = {
        (h, c): link(imgs.at[h - 1, 0, half(c)], imgs.at[h, 0, half(c)], below)
        for h in range(1, HOPS + 1)
        for c in range(2)
    }
    to_twin = {
        (h, c): link(imgs.at[h, 0, half(c)], imgs.at[h, 1, half(c)], twin)
        for h in range(HOPS + 1)
        for c in range(2)
    }
    text_y = [link(txts.at[0, 0, half(c)], txts.at[1, 0, half(c)], across) for c in range(2)]
    text_right = {
        (r, c): link(txts.at[r, 0, half(c)], txts.at[r, 3, half(c)], right)
        for r in range(2)
        for c in range(2)
    }
    text_left = {
        (r, c): link(txts.at[r, 0, half(c)], txts.at[r, 1, half(c)], left)
        for r in range(2)
        for c in range(2)
    }
    text_far_a = [link(txts.at[r, 3, half(0)], txts.at[r, 2, half(0)], right) for r in range(2)]
    text_far_b = [link(txts.at[r, 1, half(1)], txts.at[r, 2, half(1)], left) for r in range(2)]
    term = {
        (h, c): link(other_out.at[h, half(c)], other_in.at[h, half(c)], twin)
        for h in range(HOPS + 1)
        for c in range(2)
    }
    up = {
        (h, c): link(chain_out.at[h - 1, half(c)], chain_in.at[h - 1, half(c)], above)
        for h in range(1, HOPS + 1)
        for c in range(2)
    }
    far_a = [link(part_out.at[r, 2, half(0)], first_a.at[r], right) for r in range(2)]
    far_b = [link(part_out.at[r, 2, half(1)], first_b.at[r], left) for r in range(2)]
    near_right = {
        (r, c): link(part_out.at[r, 1, half(c)], second.at[r, 0, half(c)], right)
        for r in range(2)
        for c in range(2)
    }
    near_left = {
        (r, c): link(part_out.at[r, 3, half(c)], second.at[r, 1, half(c)], left)
        for r in range(2)
        for c in range(2)
    }
    over = [link(row_out.at[half(c)], row_in.at[half(c)], across) for c in range(2)]

    factor = factor_ref[0]
    shift = shift_ref[0]

    inv_img = inverse_norm(img_ref)
    imgs[0, 0] = (img_ref[...].astype(F32) * inv_img).astype(BF16)
    inv_txt = inverse_norm(txt_ref)
    txts[0, 0] = (txt_ref[...].astype(F32) * inv_txt).astype(BF16)

    pl.semaphore_wait(barrier, len(peers))

    for c in range(2):
        down[1, c].start()
        text_y[c].start()
        text_right[0, c].start()
        text_left[0, c].start()
        to_twin[0, c].start()

    def pass_on(h, c):
        down[h, c].wait_recv()
        if h < HOPS:
            down[h + 1, c].start()
        to_twin[h, c].start()

    def score(h, r):
        pictures = imgs[h].reshape(2 * ROWS, WIDE)
        words = txts[r].reshape(XS * ROWS, WIDE)
        s = lax.dot_general(
            pictures, words, (((1,), (1,)), ((), ())), preferred_element_type=F32
        )
        s = s * factor + shift
        if h == 0 and r == 0:
            rows = lax.broadcasted_iota(jnp.int32, s.shape, 0)
            cols = lax.broadcasted_iota(jnp.int32, s.shape, 1)
            positive = (rows == cols) & (rows < ROWS)
            sign = jnp.where(positive, 1.0, -1.0).astype(F32)
            value = -sign * jax.nn.sigmoid(-sign * s) * factor
        else:
            value = jax.nn.sigmoid(s) * factor
        coefs[h, :, r * XS * ROWS : (r + 1) * XS * ROWS] = value.astype(BF16)

    def image_terms(h):
        words = txts[...].reshape(2 * XS * ROWS, WIDE)
        out = jnp.dot(coefs[h], words, preferred_element_type=F32)
        grads[h] = out[:ROWS]
        other_out[h] = out[ROWS:].astype(BF16)
        for c in range(2):
            term[h, c].start()

    def climb(h, c):
        term[h, c].wait_recv()
        total = grads[h, half(c)] + other_in[h, half(c)].astype(F32)
        if h < HOPS:
            up[h + 1, c].wait_recv()
            total = total + chain_in[h, half(c)].astype(F32)
        if h > 0:
            chain_out[h - 1, half(c)] = total.astype(BF16)
            up[h, c].start()
        else:
            grads[0, half(c)] = total

    pass_on(1, 0)
    text_y[0].wait_recv()
    text_right[1, 0].start()
    text_left[1, 0].start()
    pass_on(1, 1)
    text_y[1].wait_recv()
    text_right[1, 1].start()
    text_left[1, 1].start()
    text_right[0, 0].wait_recv()
    text_far_a[0].start()
    text_left[0, 1].wait_recv()
    text_far_b[0].start()
    pass_on(2, 0)
    text_right[1, 0].wait_recv()
    text_far_a[1].start()
    pass_on(2, 1)
    text_left[1, 1].wait_recv()
    text_far_b[1].start()
    text_right[0, 1].wait_recv()
    text_left[0, 0].wait_recv()
    text_far_a[0].wait_recv()
    text_far_b[0].wait_recv()
    for c in range(2):
        to_twin[0, c].wait_recv()
    score(0, 0)
    pass_on(3, 0)
    for c in range(2):
        to_twin[1, c].wait_recv()
    score(1, 0)
    for c in range(2):
        to_twin[2, c].wait_recv()
    score(2, 0)
    text_right[1, 1].wait_recv()
    text_left[1, 0].wait_recv()
    text_far_a[1].wait_recv()
    text_far_b[1].wait_recv()
    pass_on(3, 1)
    score(0, 1)
    score(1, 1)
    score(2, 1)
    image_terms(0)
    image_terms(1)
    pass_on(4, 0)
    image_terms(2)
    for c in range(2):
        to_twin[3, c].wait_recv()
    score(3, 0)
    score(3, 1)
    image_terms(3)
    pass_on(4, 1)
    early = coefs[0:HOPS].reshape(HOPS * 2 * ROWS, 2 * XS * ROWS)
    pictures = imgs[0:HOPS].reshape(HOPS * 2 * ROWS, WIDE)
    text_sum[...] = lax.dot_general(
        early, pictures, (((0,), (0,)), ((), ())), preferred_element_type=F32
    )
    for c in range(2):
        to_twin[4, c].wait_recv()
    score(4, 0)
    score(4, 1)
    image_terms(4)

    def text_part(r, k):
        at = (r * XS + k) * ROWS
        late = coefs[HOPS, :, at : at + ROWS]
        last = imgs[HOPS].reshape(2 * ROWS, WIDE)
        extra = lax.dot_general(
            late, last, (((0,), (0,)), ((), ())), preferred_element_type=F32
        )
        total = text_sum[at : at + ROWS] + extra
        text_sum[at : at + ROWS] = total
        part_out[r, k] = total.astype(BF16)

    for r in (1, 0):
        text_part(r, 2)
        far_a[r].start()
        far_b[r].start()
    climb(4, 0)
    climb(4, 1)

    for r in (1, 0):
        text_part(r, 1)
        near_right[r, 1].start()
        text_part(r, 3)
        near_left[r, 0].start()
    text_part(1, 0)
    text_part(0, 0)

    def join(r):
        far_a[r].wait_recv()
        at = (r * XS + 1) * ROWS
        part_out[r, 1, half(0)] = (text_sum[at : at + HALF] + first_a[r].astype(F32)).astype(BF16)
        near_right[r, 0].start()
        far_b[r].wait_recv()
        at = (r * XS + 3) * ROWS + HALF
        part_out[r, 3, half(1)] = (text_sum[at : at + HALF] + first_b[r].astype(F32)).astype(BF16)
        near_left[r, 1].start()

    def row_total(r, c):
        near_right[r, c].wait_recv()
        near_left[r, c].wait_recv()
        at = r * XS * ROWS + c * HALF
        return (
            text_sum[at : at + HALF]
            + second[r, 0, half(c)].astype(F32)
            + second[r, 1, half(c)].astype(F32)
        )

    join(1)
    climb(3, 0)
    climb(3, 1)
    join(0)
    climb(2, 0)
    climb(2, 1)
    for c in range(2):
        row_out[half(c)] = row_total(1, c).astype(BF16)
        over[c].start()
    climb(1, 0)
    climb(1, 1)
    for c in range(2):
        text_sum[c * HALF : (c + 1) * HALF] = row_total(0, c)
    for c in range(2):
        over[c].wait_recv()
    txt_out[...] = back_norm(txt_ref, inv_txt, text_sum[0:ROWS] + row_in[...].astype(F32))
    climb(0, 0)
    climb(0, 1)
    img_out[...] = back_norm(img_ref, inv_img, grads[0])

    for copy in copies:
        copy.wait_send()


N_COPIES = 8 + 10 + 2 + 4 + 4 + 2 + 2 + 10 + 8 + 2 + 2 + 4 + 4 + 2


def per_device(loops, images, texts, factor, shift):
    vmem = pl.BlockSpec(memory_space=pltpu.VMEM)
    smem = pl.BlockSpec(memory_space=pltpu.SMEM)
    out = jax.ShapeDtypeStruct((ROWS, WIDE), F32)
    return pl.pallas_call(
        functools.partial(kernel, loops),
        out_shape=(out, out),
        in_specs=[smem, smem, vmem, vmem],
        out_specs=(vmem, vmem),
        scratch_shapes=[
            pltpu.VMEM((HOPS + 1, 2, ROWS, WIDE), BF16),
            pltpu.VMEM((2, XS, ROWS, WIDE), BF16),
            pltpu.VMEM((HOPS + 1, 2 * ROWS, 2 * XS * ROWS), BF16),
            pltpu.VMEM((HOPS + 1, ROWS, WIDE), F32),
            pltpu.VMEM((2 * XS * ROWS, WIDE), F32),
            pltpu.VMEM((HOPS + 1, ROWS, WIDE), BF16),
            pltpu.VMEM((HOPS + 1, ROWS, WIDE), BF16),
            pltpu.VMEM((HOPS, ROWS, WIDE), BF16),
            pltpu.VMEM((HOPS, ROWS, WIDE), BF16),
            pltpu.VMEM((2, XS, ROWS, WIDE), BF16),
            pltpu.VMEM((2, HALF, WIDE), BF16),
            pltpu.VMEM((2, HALF, WIDE), BF16),
            pltpu.VMEM((2, 2, ROWS, WIDE), BF16),
            pltpu.VMEM((ROWS, WIDE), BF16),
            pltpu.VMEM((ROWS, WIDE), BF16),
            pltpu.SemaphoreType.DMA((N_COPIES,)),
            pltpu.SemaphoreType.DMA((N_COPIES,)),
        ],
        compiler_params=pltpu.CompilerParams(
            collective_id=0, has_side_effects=True, vmem_limit_bytes=48 * 2**20
        ),
        name="siglip",
    )(factor, shift, images, texts)


def solution(mesh):
    loops = mesh.shape["loop"]
    spec = P(("grp", "loop"), None)

    def step(images, texts, factor, shift):
        return per_device(loops, images, texts, factor, shift)

    return jax.shard_map(
        step, mesh=mesh, in_specs=(spec, spec, P(), P()), out_specs=(spec, spec), check_vma=False
    )
```

time: 186 us -> 81.4 us (0.44)
  the two profiles are of different devices: /device:TPU:16 before, /device:TPU:1 now
where the time goes in v1:
time: 81.4 us; the launch traced here: 80 us
  Pallas kernels  74.7 us (92%)
  local copies, waits for them, and re-layouts  3.34 us (4%)
  between operations  1.94 us (2%)
    pallas_call x1, Pallas kernels, per_device(): pl.pallas_call(functools.partial(kernel, loops), out_shape=(out, out), in...  74.7 us
    unnamed x6, local copies, waits for them, and re-layouts  3.34 us

profile of v1, /device:TPU:1, one launch (start us, length us, event | category | flops | bytes accessed | tf_op | source)
XLA Modules:
  0.0 80.0 jit_solution(10338096969789799691)
XLA Ops:
  1.9 0.0 copy-start
  1.9 0.9 %copy-done = bf16[64,1536]{1,0:T(8,128)(2,1)S(1)} copy-done((bf16[64,1536]{1,0:T(8,128)(2,1)S(1)}, bf16[64,1536]{1,0:T(8,128)(2,1)}, u32[]{:S(2)}) %copy-start) | copy-done | bytes 196632
  2.8 0.0 copy-start.1
  2.9 0.9 %copy-done.1 = bf16[64,1536]{1,0:T(8,128)(2,1)S(1)} copy-done((bf16[64,1536]{1,0:T(8,128)(2,1)S(1)}, bf16[64,1536]{1,0:T(8,128)(2,1)}, u32[]{:S(2)}) %copy-start.1) | copy-done | bytes 196632
  3.8 74.7 %siglip.1 = (f32[64,1536]{1,0:T(8,128)S(1)}, f32[64,1536]{1,0:T(8,128)S(1)}) custom-call(f32[1]{0:T(128)S(6)} %copy.8.factor_ref, f32[1]{0:T(128)S(6)} %copy.9.shift_ref, bf16[64,1536]{1,0:T(8,128)(2,1)S(1)} %copy-done, bf16[64,1536]{1,0:T(8,128)(2,1)S(1)} %copy-done.1), custom_call_target="tpu_custom_call" | custom-call | tf_op jit(solution)/shard_map/siglip/pallas_call | solution.py:341
  78.5 0.7 copy.10
  79.2 0.7 copy.11
Async XLA Ops:
  1.9 0.9 %copy-start = (bf16[64,1536]{1,0:T(8,128)(2,1)S(1)}, bf16[64,1536]{1,0:T(8,128)(2,1)}, u32[]{:S(2)}) copy-start(bf16[64,1536]{1,0:T(8,128)(2,1)} %img_ref.1) | copy-start | bytes 589828
  2.8 0.9 %copy-start.1 = (bf16[64,1536]{1,0:T(8,128)(2,1)S(1)}, bf16[64,1536]{1,0:T(8,128)(2,1)}, u32[]{:S(2)}) copy-start(bf16[64,1536]{1,0:T(8,128)(2,1)} %txt_ref.1) | copy-start | bytes 589828

commit v2 on v1

v2 whole, which is shorter than its diff:
```python
import functools

import jax
import jax.numpy as jnp
from jax import lax
from jax.experimental import pallas as pl
from jax.experimental.pallas import tpu as pltpu
from jax.sharding import PartitionSpec as P

HOPS = 4
ROWS = 64
HALF = 32
SLICE = 16
SLICES = ROWS // SLICE
WIDE = 1536
XS = 4
ZS = 16
MINE = XS * ROWS
WORDS = 2 * MINE
MESH = pl.DeviceIdType.MESH
F32 = jnp.float32
BF16 = jnp.bfloat16
BOTH_LAST = (((1,), (1,)), ((), ()))
BOTH_FIRST = (((0,), (0,)), ((), ()))


def half(c):
    return pl.ds(c * HALF, HALF)


def sliver(u):
    return pl.ds(u * SLICE, SLICE)


def inverse_norm(ref):
    wide = ref[...].astype(F32)
    return lax.rsqrt(jnp.sum(wide * wide, axis=-1, keepdims=True) + 1e-06)


def back_norm(raw, inverse, grad):
    unit = raw.astype(F32) * inverse
    return (grad - unit * jnp.sum(unit * grad, axis=-1, keepdims=True)) * inverse


def kernel(
    loops,
    factor_ref,
    shift_ref,
    img_hbm,
    txt_hbm,
    img_out_hbm,
    txt_out_hbm,
    img_ref,
    txt_ref,
    img_out,
    txt_out,
    imgs,
    txts,
    coefs,
    grads,
    text_sum,
    other_out,
    other_in,
    chain_out,
    chain_in,
    part_out,
    first_a,
    first_b,
    second,
    row_out,
    row_in,
    load_sem,
    store_sem,
    go_sem,
    relay_down,
    relay_up,
    send_sem,
    recv_sem,
):
    g = lax.axis_index("grp")
    q = lax.axis_index("loop")
    x = g // 4
    y = (g // 2) % 2
    core = g % 2
    z = q % ZS

    def member(xx, yy, cc):
        return {"grp": xx * 4 + yy * 2 + cc, "loop": q}

    twin = member(x, y, 1 - core)
    across = member(x, 1 - y, core)
    right = member((x + 1) % XS, y, core)
    left = member((x + XS - 1) % XS, y, core)
    below = {"grp": g, "loop": (q + loops - 1) % loops}
    above = {"grp": g, "loop": (q + 1) % loops}
    first_z = z == 0
    last_z = z == ZS - 1
    far_below = {"grp": across["grp"], "loop": below["loop"]}
    far_above = {"grp": across["grp"], "loop": above["loop"]}

    loads = [
        pltpu.make_async_copy(txt_hbm, txt_ref, load_sem.at[0]),
        pltpu.make_async_copy(img_hbm, img_ref, load_sem.at[1]),
    ]
    for load in loads:
        load.start()

    barrier = pltpu.get_barrier_semaphore()
    for peer in (twin, across, right, left):
        pl.semaphore_signal(barrier, inc=1, device_id=peer, device_id_type=MESH)

    @pl.when(first_z)
    def _():
        pl.semaphore_signal(barrier, inc=1, device_id=far_below, device_id_type=MESH)

    pl.semaphore_signal(barrier, inc=1, device_id=below, device_id_type=MESH)

    @pl.when(jnp.logical_not(last_z))
    def _():
        pl.semaphore_signal(barrier, inc=1, device_id=above, device_id_type=MESH)

    used = [0]

    def remote(src, dst, device, lands=None):
        i = used[0]
        used[0] += 1
        copy = pltpu.make_async_remote_copy(
            src_ref=src,
            dst_ref=dst,
            send_sem=send_sem.at[i],
            recv_sem=recv_sem.at[i if lands is None else lands],
            device_id=device,
            device_id_type=MESH,
        )
        return i, copy

    copies = []

    def link(src, dst, device):
        copies.append(remote(src, dst, device)[1])
        return copies[-1]

    class LoopLink:
        def __init__(self, src, dst, device, at_edge, relay, onto):
            self.at_edge, self.relay = at_edge, relay
            i, self.plain = remote(src, dst, device)
            if relay is not None:
                _, self.aside = remote(src, relay, across)
                _, self.onward = remote(relay, dst, onto, lands=i)
            copies.append(self)

        def start(self):
            if self.relay is None:
                self.plain.start()
            else:
                pl.when(jnp.logical_not(self.at_edge))(self.plain.start)
                pl.when(self.at_edge)(self.aside.start)

        def send_on(self):
            self.aside.wait_recv()
            self.onward.start()

        def wait_recv(self):
            self.plain.wait_recv()

        def wait_send(self):
            if self.relay is None:
                self.plain.wait_send()
                return
            pl.when(jnp.logical_not(self.at_edge))(self.plain.wait_send)

            @pl.when(self.at_edge)
            def _():
                self.aside.wait_send()
                self.onward.wait_send()

    down = {
        (h, c): LoopLink(
            imgs.at[h - 1, 0, half(c)],
            imgs.at[h, 0, half(c)],
            below,
            first_z,
            relay_down.at[h - 1, half(c)],
            far_below,
        )
        for h in range(1, HOPS + 1)
        for c in range(2)
    }
    to_twin = {
        (h, c): link(imgs.at[h, 0, half(c)], imgs.at[h, 1, half(c)], twin)
        for h in range(HOPS + 1)
        for c in range(2)
    }
    text_y = [link(txts.at[0, 0, half(c)], txts.at[1, 0, half(c)], across) for c in range(2)]
    text_right = {
        (r, c): link(txts.at[r, 0, half(c)], txts.at[r, 3, half(c)], right)
        for r in range(2)
        for c in range(2)
    }
    text_left = {
        (r, c): link(txts.at[r, 0, half(c)], txts.at[r, 1, half(c)], left)
        for r in range(2)
        for c in range(2)
    }
    text_far_a = [link(txts.at[r, 3, half(0)], txts.at[r, 2, half(0)], right) for r in range(2)]
    text_far_b = [link(txts.at[r, 1, half(1)], txts.at[r, 2, half(1)], left) for r in range(2)]
    term = {
        (h, c): link(other_out.at[h, half(c)], other_in.at[h, half(c)], twin)
        for h in range(HOPS + 1)
        for c in range(2)
    }
    up = {
        (h, u): LoopLink(
            chain_out.at[h - 1, sliver(u)],
            chain_in.at[h - 1, sliver(u)],
            above,
            last_z,
            relay_up.at[h - 1, sliver(u)] if u % 2 else None,
            far_above,
        )
        for h in range(1, HOPS + 1)
        for u in range(SLICES)
    }
    far_a = [link(part_out.at[r, 2, half(0)], first_a.at[r], right) for r in range(2)]
    far_b = [link(part_out.at[r, 2, half(1)], first_b.at[r], left) for r in range(2)]
    near_right = {
        (r, c): link(part_out.at[r, 1, half(c)], second.at[r, 0, half(c)], right)
        for r in range(2)
        for c in range(2)
    }
    near_left = {
        (r, c): link(part_out.at[r, 3, half(c)], second.at[r, 1, half(c)], left)
        for r in range(2)
        for c in range(2)
    }
    over = [link(row_out.at[half(c)], row_in.at[half(c)], across) for c in range(2)]
    assert used[0] == N_COPIES

    factor = factor_ref[0]
    shift = shift_ref[0]

    loads[0].wait()
    inv_txt = inverse_norm(txt_ref)
    txts[0, 0] = (txt_ref[...].astype(F32) * inv_txt).astype(BF16)
    loads[1].wait()
    inv_img = inverse_norm(img_ref)
    imgs[0, 0] = (img_ref[...].astype(F32) * inv_img).astype(BF16)

    @pl.when(first_z)
    def _():
        pl.semaphore_wait(barrier, 5)

    @pl.when(jnp.logical_not(jnp.logical_or(first_z, last_z)))
    def _():
        pl.semaphore_wait(barrier, 6)

    @pl.when(last_z)
    def _():
        pl.semaphore_wait(barrier, 7)
        pl.semaphore_signal(go_sem, inc=1, device_id=far_above, device_id_type=MESH)

    for c in range(2):
        text_y[c].start()
        pl.when(jnp.logical_not(first_z))(down[1, c].start)
        text_right[0, c].start()
        text_left[0, c].start()
    for c in range(2):
        to_twin[0, c].start()

    def pass_on(h, c):
        down[h, c].wait_recv()
        if h < HOPS:
            down[h + 1, c].start()
        to_twin[h, c].start()

    def send_on(links, at_edge, *keys):
        @pl.when(at_edge)
        def _():
            for key in keys:
                links[key].send_on()

    down_on = functools.partial(send_on, down, first_z)
    up_on = functools.partial(send_on, up, last_z)

    def from_twin(h):
        for c in range(2):
            to_twin[h, c].wait_recv()

    def spread_row(c):
        text_y[c].wait_recv()
        text_right[1, c].start()
        text_left[1, c].start()

    def coef_of(s):
        return jax.nn.sigmoid(s * factor + shift) * factor

    def scores(pictures):
        return lax.dot_general(
            pictures, txts[...].reshape(WORDS, WIDE), BOTH_LAST, preferred_element_type=F32
        )

    def coef_hops(lo, hi):
        s = scores(imgs[lo:hi].reshape((hi - lo) * 2 * ROWS, WIDE))
        coefs[lo:hi] = coef_of(s).astype(BF16).reshape(hi - lo, 2, ROWS, WORDS)
        if lo == 0:
            own = s[0:ROWS, 0:128] * factor + shift
            rows = lax.broadcasted_iota(jnp.int32, own.shape, 0)
            cols = lax.broadcasted_iota(jnp.int32, own.shape, 1)
            sign = jnp.where(rows == cols, 1.0, -1.0).astype(F32)
            value = -sign * jax.nn.sigmoid(-sign * own) * factor
            coefs[0, 0, :, 0:128] = value.astype(BF16)

    def coef_half(h, c):
        s = scores(imgs[h, :, c * HALF : (c + 1) * HALF].reshape(2 * HALF, WIDE))
        coefs[h, :, c * HALF : (c + 1) * HALF] = coef_of(s).astype(BF16).reshape(2, HALF, WORDS)

    def terms_hops(lo, hi):
        out = jnp.dot(
            coefs[lo:hi].reshape((hi - lo) * 2 * ROWS, WORDS),
            txts[...].reshape(WORDS, WIDE),
            preferred_element_type=F32,
        ).reshape(hi - lo, 2, ROWS, WIDE)
        grads[lo:hi] = out[:, 0]
        other_out[lo:hi] = out[:, 1].astype(BF16)
        for h in range(lo, hi):
            for c in range(2):
                term[h, c].start()

    def terms_half(h, c):
        out = jnp.dot(
            coefs[h, :, c * HALF : (c + 1) * HALF].reshape(2 * HALF, WORDS),
            txts[...].reshape(WORDS, WIDE),
            preferred_element_type=F32,
        ).reshape(2, HALF, WIDE)
        grads[h, half(c)] = out[0]
        other_out[h, half(c)] = out[1].astype(BF16)
        term[h, c].start()

    def climb(h, u):
        if u % 2 == 0:
            term[h, u // 2].wait_recv()
        total = grads[h, sliver(u)] + other_in[h, sliver(u)].astype(F32)
        if h < HOPS:
            up[h + 1, u].wait_recv()
            total = total + chain_in[h, sliver(u)].astype(F32)
        if h > 0:
            chain_out[h - 1, sliver(u)] = total.astype(BF16)
            up[h, u].start()
        else:
            grads[0, sliver(u)] = total

    spread_row(0)

    pl.when(first_z)(down[1, 0].start)
    pass_on(1, 0)
    spread_row(1)
    pl.when(first_z)(down[1, 1].start)
    text_right[0, 0].wait_recv()
    text_far_a[0].start()
    text_left[0, 1].wait_recv()
    text_far_b[0].start()
    pass_on(1, 1)

    @pl.when(first_z)
    def _():
        pl.semaphore_wait(go_sem, 1)

    down_on((1, 0), (1, 1))

    def far_text(side):
        (text_right[1, 0] if side == 0 else text_left[1, 1]).wait_recv()
        (text_far_a[1] if side == 0 else text_far_b[1]).start()

    pl.when(last_z)(functools.partial(far_text, 0))
    pass_on(2, 0)
    pl.when(jnp.logical_not(last_z))(functools.partial(far_text, 0))
    pl.when(last_z)(functools.partial(far_text, 1))
    pass_on(2, 1)
    pl.when(jnp.logical_not(last_z))(functools.partial(far_text, 1))

    down_on((2, 0), (2, 1))
    pass_on(3, 0)
    down_on((3, 0))
    pass_on(3, 1)
    down_on((3, 1))
    text_right[0, 1].wait_recv()
    text_left[0, 0].wait_recv()
    text_right[1, 1].wait_recv()
    text_left[1, 0].wait_recv()
    for r in range(2):
        text_far_a[r].wait_recv()
        text_far_b[r].wait_recv()
    for h in range(2):
        from_twin(h)
    coef_hops(0, 2)
    pass_on(4, 0)
    down_on((4, 0))
    for h in range(2, 4):
        from_twin(h)
    coef_hops(2, 4)
    down_on((4, 1))
    to_twin[4, 0].wait_recv()
    coef_half(4, 0)
    terms_half(4, 0)
    pass_on(4, 1)
    terms_hops(0, 4)
    climb(4, 0)
    climb(4, 1)

    def text_row(r, lo, hi):
        at = r * MINE
        total = lax.dot_general(
            coefs[lo:hi, :, :, at : at + MINE].reshape((hi - lo) * 2 * ROWS, MINE),
            imgs[lo:hi].reshape((hi - lo) * 2 * ROWS, WIDE),
            BOTH_FIRST,
            preferred_element_type=F32,
        )
        if lo > 0:
            total = text_sum[at : at + MINE] + total
        text_sum[at : at + MINE] = total
        if hi > HOPS:
            part_out[r] = total.astype(BF16).reshape(XS, ROWS, WIDE)

    def join(r):
        far_a[r].wait_recv()
        at = (r * XS + 1) * ROWS
        part_out[r, 1, half(0)] = (text_sum[at : at + HALF] + first_a[r].astype(F32)).astype(BF16)
        near_right[r, 0].start()
        far_b[r].wait_recv()
        at = (r * XS + 3) * ROWS + HALF
        part_out[r, 3, half(1)] = (text_sum[at : at + HALF] + first_b[r].astype(F32)).astype(BF16)
        near_left[r, 1].start()

    def row_total(r, c):
        near_right[r, c].wait_recv()
        near_left[r, c].wait_recv()
        at = r * MINE + c * HALF
        return (
            text_sum[at : at + HALF]
            + second[r, 0, half(c)].astype(F32)
            + second[r, 1, half(c)].astype(F32)
        )

    def join_rows():
        join(1)
        near_right[0, 1].start()
        near_left[0, 0].start()

    def store(ref, hbm, rows, i):
        copy = pltpu.make_async_copy(ref.at[rows], hbm.at[rows], store_sem.at[i])
        copy.start()
        return copy

    def image_result(c):
        rows = slice(c * HALF, (c + 1) * HALF)
        img_out[rows] = back_norm(img_ref[rows], inv_img[rows], grads[0, rows])
        return store(img_out, img_out_hbm, half(c), c)

    text_row(1, 0, HOPS)
    to_twin[4, 1].wait_recv()
    coef_half(4, 1)
    text_row(1, HOPS, HOPS + 1)
    far_a[1].start()
    far_b[1].start()
    near_right[1, 1].start()
    near_left[1, 0].start()
    terms_half(4, 1)
    text_row(0, 0, HOPS + 1)
    far_a[0].start()
    far_b[0].start()
    up_on((4, 1))
    climb(4, 2)
    climb(4, 3)

    def sum_row():
        for c in range(2):
            row_out[half(c)] = row_total(1, c).astype(BF16)
            over[c].start()

    def own_row():
        for c in range(2):
            text_sum[c * HALF : (c + 1) * HALF] = row_total(0, c)

    steps = (join_rows, functools.partial(join, 0), sum_row, own_row)

    usual = (1, 2, 3, 4)
    moved = ({0: 0}, {0: 0, 1: 1}, {0: 1, 1: 2, 2: 2, ZS - 1: 4}, {0: 2, 1: 3, 2: 3, 3: 3})

    def at_place(place):
        for step, common, others in zip(steps, usual, moved):
            if place == common:
                here = functools.reduce(jnp.logical_and, [z != at for at in others if others[at] != place])
                pl.when(here)(step)
            else:
                chosen = [z == at for at in others if others[at] == place]
                if chosen:
                    pl.when(functools.reduce(jnp.logical_or, chosen))(step)

    at_place(0)
    climb(3, 0)
    climb(3, 1)
    at_place(1)
    up_on((4, 3), (3, 1))
    climb(2, 0)
    climb(2, 1)
    climb(3, 2)
    climb(3, 3)
    at_place(2)
    up_on((2, 1), (3, 3))
    climb(1, 0)
    climb(1, 1)
    climb(2, 2)
    climb(2, 3)
    at_place(3)
    up_on((1, 1))
    climb(0, 0)
    climb(0, 1)
    stores = [image_result(0)]
    up_on((2, 3))
    climb(1, 2)
    climb(1, 3)
    up_on((1, 3))
    at_place(4)
    for c in range(2):
        over[c].wait_recv()
    txt_out[...] = back_norm(txt_ref[...], inv_txt, text_sum[0:ROWS] + row_in[...].astype(F32))
    stores.append(store(txt_out, txt_out_hbm, pl.ds(0, ROWS), 2))
    climb(0, 2)
    climb(0, 3)
    stores.append(image_result(1))

    for copy in copies:
        copy.wait_send()
    for copy in stores:
        copy.wait()


N_COPIES = 3 * 8 + 10 + 2 + 4 + 4 + 2 + 2 + 10 + 2 * 16 + 2 + 2 + 4 + 4 + 2


def per_device(loops, images, texts, factor, shift):
    smem = pl.BlockSpec(memory_space=pltpu.SMEM)
    hbm = pl.BlockSpec(memory_space=pl.ANY)
    out = jax.ShapeDtypeStruct((ROWS, WIDE), F32)
    return pl.pallas_call(
        functools.partial(kernel, loops),
        out_shape=(out, out),
        in_specs=[smem, smem, hbm, hbm],
        out_specs=(hbm, hbm),
        scratch_shapes=[
            pltpu.VMEM((ROWS, WIDE), BF16),
            pltpu.VMEM((ROWS, WIDE), BF16),
            pltpu.VMEM((ROWS, WIDE), F32),
            pltpu.VMEM((ROWS, WIDE), F32),
            pltpu.VMEM((HOPS + 1, 2, ROWS, WIDE), BF16),
            pltpu.VMEM((2, XS, ROWS, WIDE), BF16),
            pltpu.VMEM((HOPS + 1, 2, ROWS, WORDS), BF16),
            pltpu.VMEM((HOPS + 1, ROWS, WIDE), F32),
            pltpu.VMEM((WORDS, WIDE), F32),
            pltpu.VMEM((HOPS + 1, ROWS, WIDE), BF16),
            pltpu.VMEM((HOPS + 1, ROWS, WIDE), BF16),
            pltpu.VMEM((HOPS, ROWS, WIDE), BF16),
            pltpu.VMEM((HOPS, ROWS, WIDE), BF16),
            pltpu.VMEM((2, XS, ROWS, WIDE), BF16),
            pltpu.VMEM((2, HALF, WIDE), BF16),
            pltpu.VMEM((2, HALF, WIDE), BF16),
            pltpu.VMEM((2, 2, ROWS, WIDE), BF16),
            pltpu.VMEM((ROWS, WIDE), BF16),
            pltpu.VMEM((ROWS, WIDE), BF16),
            pltpu.SemaphoreType.DMA((2,)),
            pltpu.SemaphoreType.DMA((3,)),
            pltpu.SemaphoreType.REGULAR,
            pltpu.VMEM((HOPS, ROWS, WIDE), BF16),
            pltpu.VMEM((HOPS, ROWS, WIDE), BF16),
            pltpu.SemaphoreType.DMA((N_COPIES,)),
            pltpu.SemaphoreType.DMA((N_COPIES,)),
        ],
        compiler_params=pltpu.CompilerParams(
            collective_id=0, has_side_effects=True, vmem_limit_bytes=60 * 2**20
        ),
        name="siglip",
    )(factor, shift, images, texts)


def solution(mesh):
    loops = mesh.shape["loop"]
    spec = P(("grp", "loop"), None)

    def step(images, texts, factor, shift):
        return per_device(loops, images, texts, factor, shift)

    return jax.shard_map(
        step, mesh=mesh, in_specs=(spec, spec, P(), P()), out_specs=(spec, spec), check_vma=False
    )
```

time: 81.4 us -> 71.4 us (0.88)
  Pallas kernels: 74.7 us -> 66.1 us
    pallas_call x1, Pallas kernels: 74.7 us -> 66.1 us  [per_device(): pl.pallas_call(functools.partial(kernel, loops), out_shape=(out, out), in...]
    unnamed x6 -> x4, local copies, waits for them, and re-layouts: 3.34 us -> 2.57 us
where the time goes in v2:
time: 71.4 us; the launch traced here: 70.6 us
  Pallas kernels  66.1 us (93%)
  local copies, waits for them, and re-layouts  2.57 us (4%)
  between operations  1.94 us (3%)
    pallas_call x1, Pallas kernels, per_device(): pl.pallas_call(functools.partial(kernel, loops), out_shape=(out, out), in...  66.1 us
    unnamed x4, local copies, waits for them, and re-layouts  2.57 us

profile of v2, /device:TPU:1, one launch (start us, length us, event | category | flops | bytes accessed | tf_op | source)
XLA Modules:
  0.0 70.6 jit_solution(15035595457895355425)
XLA Ops:
  1.9 66.1 %siglip.1 = (f32[64,1536]{1,0:T(8,128)}, f32[64,1536]{1,0:T(8,128)}) custom-call(f32[1]{0:T(128)S(6)} %copy.8.factor_ref, f32[1]{0:T(128)S(6)} %copy.9.shift_ref, bf16[64,1536]{1,0:T(8,128)(2,1)} %img_hbm.1, bf16[64,1536]{1,0:T(8,128)(2,1)} %txt_hbm.1), custom_call_target="tpu_custom_call" | custom-call | tf_op jit(solution)/shard_map/siglip/pallas_call | solution.py:545
  68.1 0.0 copy-start
  68.1 1.8 %copy.10 = f32[64,1536]{1,0:T(8,128)} copy(f32[64,1536]{1,0:T(8,128)} %get-tuple-element.4) | data formatting | bytes 786432
  69.9 0.0 copy-done
  69.9 0.7 %copy.11 = f32[64,1536]{1,0:T(8,128)} copy(f32[64,1536]{1,0:T(8,128)S(1)} %copy-done) | data formatting | bytes 786432
Async XLA Ops:
  68.1 1.8 %copy-start = (f32[64,1536]{1,0:T(8,128)S(1)}, f32[64,1536]{1,0:T(8,128)}, u32[]{:S(2)}) copy-start(f32[64,1536]{1,0:T(8,128)} %get-tuple-element.5) | copy-start | bytes 1179652

commit v3 on v2

--- a/solution.py
+++ b/solution.py
@@ -48,12 +48,10 @@
     shift_ref,
     img_hbm,
     txt_hbm,
-    img_out_hbm,
-    txt_out_hbm,
+    img_out,
+    txt_out,
     img_ref,
     txt_ref,
-    img_out,
-    txt_out,
     imgs,
     txts,
     coefs,
@@ -70,7 +68,6 @@
     row_out,
     row_in,
     load_sem,
-    store_sem,
     go_sem,
     relay_down,
     relay_up,
@@ -239,6 +236,11 @@
     factor = factor_ref[0]
     shift = shift_ref[0]
 
+    @pl.when(last_z)
+    def _():
+        pl.semaphore_wait(barrier, 7)
+        pl.semaphore_signal(go_sem, inc=1, device_id=far_above, device_id_type=MESH)
+
     loads[0].wait()
     inv_txt = inverse_norm(txt_ref)
     txts[0, 0] = (txt_ref[...].astype(F32) * inv_txt).astype(BF16)
@@ -254,22 +256,21 @@
     def _():
         pl.semaphore_wait(barrier, 6)
 
-    @pl.when(last_z)
-    def _():
-        pl.semaphore_wait(barrier, 7)
-        pl.semaphore_signal(go_sem, inc=1, device_id=far_above, device_id_type=MESH)
-
     for c in range(2):
         text_y[c].start()
         pl.when(jnp.logical_not(first_z))(down[1, c].start)
         text_right[0, c].start()
         text_left[0, c].start()
     for c in range(2):
+        pl.when(first_z)(down[1, c].start)
+    for c in range(2):
         to_twin[0, c].start()
 
     def pass_on(h, c):
         down[h, c].wait_recv()
-        if h < HOPS:
+        if h == 1:
+            pl.when(jnp.logical_not(first_z))(down[2, c].start)
+        elif h < HOPS:
             down[h + 1, c].start()
         to_twin[h, c].start()
 
@@ -351,10 +352,8 @@
 
     spread_row(0)
 
-    pl.when(first_z)(down[1, 0].start)
     pass_on(1, 0)
     spread_row(1)
-    pl.when(first_z)(down[1, 1].start)
     text_right[0, 0].wait_recv()
     text_far_a[0].start()
     text_left[0, 1].wait_recv()
@@ -363,9 +362,11 @@
 
     @pl.when(first_z)
     def _():
+        down[2, 0].start()
         pl.semaphore_wait(go_sem, 1)
 
     down_on((1, 0), (1, 1))
+    pl.when(first_z)(down[2, 1].start)
 
     def far_text(side):
         (text_right[1, 0] if side == 0 else text_left[1, 1]).wait_recv()
@@ -407,19 +408,16 @@
     climb(4, 0)
     climb(4, 1)
 
-    def text_row(r, lo, hi):
+    def text_row(r):
         at = r * MINE
         total = lax.dot_general(
-            coefs[lo:hi, :, :, at : at + MINE].reshape((hi - lo) * 2 * ROWS, MINE),
-            imgs[lo:hi].reshape((hi - lo) * 2 * ROWS, WIDE),
+            coefs[:, :, :, at : at + MINE].reshape((HOPS + 1) * 2 * ROWS, MINE),
+            imgs[...].reshape((HOPS + 1) * 2 * ROWS, WIDE),
             BOTH_FIRST,
             preferred_element_type=F32,
         )
-        if lo > 0:
-            total = text_sum[at : at + MINE] + total
         text_sum[at : at + MINE] = total
-        if hi > HOPS:
-            part_out[r] = total.astype(BF16).reshape(XS, ROWS, WIDE)
+        part_out[r] = total.astype(BF16).reshape(XS, ROWS, WIDE)
 
     def join(r):
         far_a[r].wait_recv()
@@ -446,31 +444,24 @@
         near_right[0, 1].start()
         near_left[0, 0].start()
 
-    def store(ref, hbm, rows, i):
-        copy = pltpu.make_async_copy(ref.at[rows], hbm.at[rows], store_sem.at[i])
-        copy.start()
-        return copy
-
     def image_result(c):
         rows = slice(c * HALF, (c + 1) * HALF)
         img_out[rows] = back_norm(img_ref[rows], inv_img[rows], grads[0, rows])
-        return store(img_out, img_out_hbm, half(c), c)
-
-    text_row(1, 0, HOPS)
+
     to_twin[4, 1].wait_recv()
     coef_half(4, 1)
-    text_row(1, HOPS, HOPS + 1)
+    terms_half(4, 1)
+    text_row(1)
     far_a[1].start()
     far_b[1].start()
     near_right[1, 1].start()
     near_left[1, 0].start()
-    terms_half(4, 1)
-    text_row(0, 0, HOPS + 1)
-    far_a[0].start()
-    far_b[0].start()
     up_on((4, 1))
     climb(4, 2)
     climb(4, 3)
+    text_row(0)
+    far_a[0].start()
+    far_b[0].start()
 
     def sum_row():
         for c in range(2):
@@ -500,39 +491,36 @@
     climb(3, 0)
     climb(3, 1)
     at_place(1)
+    climb(3, 2)
+    climb(3, 3)
     up_on((4, 3), (3, 1))
     climb(2, 0)
     climb(2, 1)
-    climb(3, 2)
-    climb(3, 3)
     at_place(2)
-    up_on((2, 1), (3, 3))
+    up_on((3, 3))
+    climb(2, 2)
+    climb(2, 3)
+    up_on((2, 1))
     climb(1, 0)
     climb(1, 1)
-    climb(2, 2)
-    climb(2, 3)
     at_place(3)
-    up_on((1, 1))
+    climb(1, 2)
+    climb(1, 3)
+    up_on((2, 3), (1, 1))
     climb(0, 0)
     climb(0, 1)
-    stores = [image_result(0)]
-    up_on((2, 3))
-    climb(1, 2)
-    climb(1, 3)
+    image_result(0)
     up_on((1, 3))
     at_place(4)
     for c in range(2):
         over[c].wait_recv()
     txt_out[...] = back_norm(txt_ref[...], inv_txt, text_sum[0:ROWS] + row_in[...].astype(F32))
-    stores.append(store(txt_out, txt_out_hbm, pl.ds(0, ROWS), 2))
     climb(0, 2)
     climb(0, 3)
-    stores.append(image_result(1))
+    image_result(1)
 
     for copy in copies:
         copy.wait_send()
-    for copy in stores:
-        copy.wait()
 
 
 N_COPIES = 3 * 8 + 10 + 2 + 4 + 4 + 2 + 2 + 10 + 2 * 16 + 2 + 2 + 4 + 4 + 2
@@ -540,18 +528,17 @@
 
 def per_device(loops, images, texts, factor, shift):
     smem = pl.BlockSpec(memory_space=pltpu.SMEM)
-    hbm = pl.BlockSpec(memory_space=pl.ANY)
+    hbm = pl.BlockSpec(memory_space=pltpu.HBM)
+    vmem = pl.BlockSpec(memory_space=pltpu.VMEM)
     out = jax.ShapeDtypeStruct((ROWS, WIDE), F32)
     return pl.pallas_call(
         functools.partial(kernel, loops),
         out_shape=(out, out),
         in_specs=[smem, smem, hbm, hbm],
-        out_specs=(hbm, hbm),
+        out_specs=(vmem, vmem),
         scratch_shapes=[
             pltpu.VMEM((ROWS, WIDE), BF16),
             pltpu.VMEM((ROWS, WIDE), BF16),
-            pltpu.VMEM((ROWS, WIDE), F32),
-            pltpu.VMEM((ROWS, WIDE), F32),
             pltpu.VMEM((HOPS + 1, 2, ROWS, WIDE), BF16),
             pltpu.VMEM((2, XS, ROWS, WIDE), BF16),
             pltpu.VMEM((HOPS + 1, 2, ROWS, WORDS), BF16),
@@ -568,7 +555,6 @@
             pltpu.VMEM((ROWS, WIDE), BF16),
             pltpu.VMEM((ROWS, WIDE), BF16),
             pltpu.SemaphoreType.DMA((2,)),
-            pltpu.SemaphoreType.DMA((3,)),
             pltpu.SemaphoreType.REGULAR,
             pltpu.VMEM((HOPS, ROWS, WIDE), BF16),
             pltpu.VMEM((HOPS, ROWS, WIDE), BF16),
@@ -576,10 +562,15 @@
             pltpu.SemaphoreType.DMA((N_COPIES,)),
         ],
         compiler_params=pltpu.CompilerParams(
-            collective_id=0, has_side_effects=True, vmem_limit_bytes=60 * 2**20
+            collective_id=0, has_side_effects=True, vmem_limit_bytes=48 * 2**20
         ),
         name="siglip",
-    )(factor, shift, images, texts)
+    )(
+        factor,
+        shift,
+        pltpu.with_memory_space_constraint(images, pltpu.HBM),
+        pltpu.with_memory_space_constraint(texts, pltpu.HBM),
+    )
 
 
 def solution(mesh):

time: 71.4 us -> 66.2 us (0.927)
  Pallas kernels: 66.1 us -> 62.3 us
  local copies, waits for them, and re-layouts: 2.57 us -> 1.49 us
    pallas_call x1, Pallas kernels: 66.1 us -> 62.3 us  [per_device(): pl.pallas_call(functools.partial(kernel, loops), out_shape=(out, out), in...]
    unnamed x4 -> x2, local copies, waits for them, and re-layouts: 2.57 us -> 1.49 us
where the time goes in v3:
time: 66.2 us; the launch traced here: 65.7 us
  Pallas kernels  62.3 us (94%)
  between operations  1.93 us (3%)
  local copies, waits for them, and re-layouts  1.49 us (2%)
    pallas_call x1, Pallas kernels, per_device(): pl.pallas_call(functools.partial(kernel, loops), out_shape=(out, out), in...  62.3 us
    unnamed x2, local copies, waits for them, and re-layouts  1.49 us

profile of v3, /device:TPU:1, one launch (start us, length us, event | category | flops | bytes accessed | tf_op | source)
XLA Modules:
  0.0 65.7 jit_solution(17621000101715033537)
XLA Ops:
  1.9 62.3 %siglip.1 = (f32[64,1536]{1,0:T(8,128)S(1)}, f32[64,1536]{1,0:T(8,128)S(1)}) custom-call(f32[1]{0:T(128)S(6)} %copy.8.factor_ref, f32[1]{0:T(128)S(6)} %copy.9.shift_ref, bf16[64,1536]{1,0:T(8,128)(2,1)} %img_hbm.1, bf16[64,1536]{1,0:T(8,128)(2,1)} %txt_hbm.1), custom_call_target="tpu_custom_call" | custom-call | tf_op jit(solution)/shard_map/siglip/pallas_call | solution.py:534
  64.2 0.7 %copy.10 = f32[64,1536]{1,0:T(8,128)} copy(f32[64,1536]{1,0:T(8,128)S(1)} %get-tuple-element.4) | data formatting | bytes 786432
  65.0 0.7 %copy.11 = f32[64,1536]{1,0:T(8,128)} copy(f32[64,1536]{1,0:T(8,128)S(1)} %get-tuple-element.5) | data formatting | bytes 786432

commit v4 on v3

--- a/solution.py
+++ b/solution.py
@@ -17,6 +17,8 @@
 ZS = 16
 MINE = XS * ROWS
 WORDS = 2 * MINE
+DOWN, UP, TWIN, TEXT, PART = 0, 2, 4, 5, 6
+N_LEAVES = 7
 MESH = pl.DeviceIdType.MESH
 F32 = jnp.float32
 BF16 = jnp.bfloat16
@@ -118,33 +120,31 @@
 
     used = [0]
 
-    def remote(src, dst, device, lands=None):
-        i = used[0]
+    def arrival():
         used[0] += 1
-        copy = pltpu.make_async_remote_copy(
+        return used[0] - 1
+
+    def remote(src, dst, device, leaves, lands):
+        return pltpu.make_async_remote_copy(
             src_ref=src,
             dst_ref=dst,
-            send_sem=send_sem.at[i],
-            recv_sem=recv_sem.at[i if lands is None else lands],
+            send_sem=send_sem.at[leaves],
+            recv_sem=recv_sem.at[lands],
             device_id=device,
             device_id_type=MESH,
         )
-        return i, copy
-
-    copies = []
-
-    def link(src, dst, device):
-        copies.append(remote(src, dst, device)[1])
-        return copies[-1]
+
+    def link(src, dst, device, leaves, lands=None):
+        return remote(src, dst, device, leaves, arrival() if lands is None else lands)
 
     class LoopLink:
-        def __init__(self, src, dst, device, at_edge, relay, onto):
+        def __init__(self, src, dst, device, leaves, at_edge, relay, onto):
             self.at_edge, self.relay = at_edge, relay
-            i, self.plain = remote(src, dst, device)
+            lands = arrival()
+            self.plain = remote(src, dst, device, leaves, lands)
             if relay is not None:
-                _, self.aside = remote(src, relay, across)
-                _, self.onward = remote(relay, dst, onto, lands=i)
-            copies.append(self)
+                self.aside = remote(src, relay, across, leaves, arrival())
+                self.onward = remote(relay, dst, onto, leaves + 1, lands)
 
         def start(self):
             if self.relay is None:
@@ -160,22 +160,12 @@
         def wait_recv(self):
             self.plain.wait_recv()
 
-        def wait_send(self):
-            if self.relay is None:
-                self.plain.wait_send()
-                return
-            pl.when(jnp.logical_not(self.at_edge))(self.plain.wait_send)
-
-            @pl.when(self.at_edge)
-            def _():
-                self.aside.wait_send()
-                self.onward.wait_send()
-
     down = {
         (h, c): LoopLink(
             imgs.at[h - 1, 0, half(c)],
             imgs.at[h, 0, half(c)],
             below,
+            DOWN,
             first_z,
             relay_down.at[h - 1, half(c)],
             far_below,
@@ -183,55 +173,91 @@
         for h in range(1, HOPS + 1)
         for c in range(2)
     }
-    to_twin = {
-        (h, c): link(imgs.at[h, 0, half(c)], imgs.at[h, 1, half(c)], twin)
-        for h in range(HOPS + 1)
-        for c in range(2)
-    }
-    text_y = [link(txts.at[0, 0, half(c)], txts.at[1, 0, half(c)], across) for c in range(2)]
+    to_twin = [link(imgs.at[0, 0], imgs.at[0, 1], twin, TWIN)]
+    to_twin_half = {}
+    for h in range(1, HOPS + 1):
+        lands = arrival()
+        for c in range(2):
+            alone = lands if h < HOPS or c == 0 else arrival()
+            to_twin_half[h, c] = link(
+                imgs.at[h, 0, half(c)], imgs.at[h, 1, half(c)], twin, TWIN, alone
+            )
+        if h < HOPS:
+            to_twin.append(link(imgs.at[h, 0], imgs.at[h, 1], twin, TWIN, lands))
+    text_y = [
+        link(txts.at[0, 0, half(c)], txts.at[1, 0, half(c)], across, TEXT) for c in range(2)
+    ]
+    text_last = arrival()
     text_right = {
-        (r, c): link(txts.at[r, 0, half(c)], txts.at[r, 3, half(c)], right)
+        (r, c): link(
+            txts.at[r, 0, half(c)],
+            txts.at[r, 3, half(c)],
+            right,
+            TEXT,
+            arrival() if c == 0 else text_last,
+        )
         for r in range(2)
         for c in range(2)
     }
     text_left = {
-        (r, c): link(txts.at[r, 0, half(c)], txts.at[r, 1, half(c)], left)
+        (r, c): link(
+            txts.at[r, 0, half(c)],
+            txts.at[r, 1, half(c)],
+            left,
+            TEXT,
+            arrival() if c == 1 else text_last,
+        )
         for r in range(2)
         for c in range(2)
     }
-    text_far_a = [link(txts.at[r, 3, half(0)], txts.at[r, 2, half(0)], right) for r in range(2)]
-    text_far_b = [link(txts.at[r, 1, half(1)], txts.at[r, 2, half(1)], left) for r in range(2)]
-    term = {
-        (h, c): link(other_out.at[h, half(c)], other_in.at[h, half(c)], twin)
-        for h in range(HOPS + 1)
-        for c in range(2)
-    }
+    text_far_a = [
+        link(txts.at[r, 3, half(0)], txts.at[r, 2, half(0)], right, TEXT, text_last)
+        for r in range(2)
+    ]
+    text_far_b = [
+        link(txts.at[r, 1, half(1)], txts.at[r, 2, half(1)], left, TEXT, text_last)
+        for r in range(2)
+    ]
+    text_rest = link(txts.at[0], txts.at[0], right, TEXT, text_last)
+    term_early = link(other_out.at[0:HOPS], other_in.at[0:HOPS], twin, TWIN)
+    term_last = [
+        link(other_out.at[HOPS, half(c)], other_in.at[HOPS, half(c)], twin, TWIN) for c in range(2)
+    ]
     up = {
         (h, u): LoopLink(
             chain_out.at[h - 1, sliver(u)],
             chain_in.at[h - 1, sliver(u)],
             above,
+            UP,
             last_z,
-            relay_up.at[h - 1, sliver(u)] if u % 2 else None,
+            relay_up.at[h - 2, u // 2] if u % 2 and h > 1 else None,
             far_above,
         )
         for h in range(1, HOPS + 1)
         for u in range(SLICES)
     }
-    far_a = [link(part_out.at[r, 2, half(0)], first_a.at[r], right) for r in range(2)]
-    far_b = [link(part_out.at[r, 2, half(1)], first_b.at[r], left) for r in range(2)]
+    far_a = [link(part_out.at[r, 2, half(0)], first_a.at[r], right, PART) for r in range(2)]
+    far_b = [link(part_out.at[r, 2, half(1)], first_b.at[r], left, PART) for r in range(2)]
+    row_lands = [arrival() for _ in range(2)]
     near_right = {
-        (r, c): link(part_out.at[r, 1, half(c)], second.at[r, 0, half(c)], right)
+        (r, c): link(
+            part_out.at[r, 1, half(c)], second.at[r, 0, half(c)], right, PART, row_lands[r]
+        )
         for r in range(2)
         for c in range(2)
     }
     near_left = {
-        (r, c): link(part_out.at[r, 3, half(c)], second.at[r, 1, half(c)], left)
+        (r, c): link(
+            part_out.at[r, 3, half(c)], second.at[r, 1, half(c)], left, PART, row_lands[r]
+        )
         for r in range(2)
         for c in range(2)
     }
-    over = [link(row_out.at[half(c)], row_in.at[half(c)], across) for c in range(2)]
-    assert used[0] == N_COPIES
+    near_rows = [link(second.at[r], second.at[r], right, PART, row_lands[r]) for r in range(2)]
+    over_lands = arrival()
+    over = [link(row_out.at[half(c)], row_in.at[half(c)], across, TEXT, over_lands) for c in range(2)]
+    over_all = link(row_out, row_in, across, TEXT, over_lands)
+    assert used[0] == N_ARRIVALS, used[0]
 
     factor = factor_ref[0]
     shift = shift_ref[0]
@@ -263,8 +289,7 @@
         text_left[0, c].start()
     for c in range(2):
         pl.when(first_z)(down[1, c].start)
-    for c in range(2):
-        to_twin[0, c].start()
+    to_twin[0].start()
 
     def pass_on(h, c):
         down[h, c].wait_recv()
@@ -272,7 +297,7 @@
             pl.when(jnp.logical_not(first_z))(down[2, c].start)
         elif h < HOPS:
             down[h + 1, c].start()
-        to_twin[h, c].start()
+        to_twin_half[h, c].start()
 
     def send_on(links, at_edge, *keys):
         @pl.when(at_edge)
@@ -284,8 +309,7 @@
     up_on = functools.partial(send_on, up, last_z)
 
     def from_twin(h):
-        for c in range(2):
-            to_twin[h, c].wait_recv()
+        to_twin[h].wait_recv()
 
     def spread_row(c):
         text_y[c].wait_recv()
@@ -323,9 +347,7 @@
         ).reshape(hi - lo, 2, ROWS, WIDE)
         grads[lo:hi] = out[:, 0]
         other_out[lo:hi] = out[:, 1].astype(BF16)
-        for h in range(lo, hi):
-            for c in range(2):
-                term[h, c].start()
+        term_early.start()
 
     def terms_half(h, c):
         out = jnp.dot(
@@ -335,11 +357,13 @@
         ).reshape(2, HALF, WIDE)
         grads[h, half(c)] = out[0]
         other_out[h, half(c)] = out[1].astype(BF16)
-        term[h, c].start()
+        term_last[c].start()
 
     def climb(h, u):
-        if u % 2 == 0:
-            term[h, u // 2].wait_recv()
+        if h == HOPS and u % 2 == 0:
+            term_last[u // 2].wait_recv()
+        if h == HOPS - 1 and u == 0:
+            term_early.wait_recv()
         total = grads[h, sliver(u)] + other_in[h, sliver(u)].astype(F32)
         if h < HOPS:
             up[h + 1, u].wait_recv()
@@ -384,13 +408,7 @@
     down_on((3, 0))
     pass_on(3, 1)
     down_on((3, 1))
-    text_right[0, 1].wait_recv()
-    text_left[0, 0].wait_recv()
-    text_right[1, 1].wait_recv()
-    text_left[1, 0].wait_recv()
-    for r in range(2):
-        text_far_a[r].wait_recv()
-        text_far_b[r].wait_recv()
+    text_rest.wait_recv()
     for h in range(2):
         from_twin(h)
     coef_hops(0, 2)
@@ -400,7 +418,7 @@
         from_twin(h)
     coef_hops(2, 4)
     down_on((4, 1))
-    to_twin[4, 0].wait_recv()
+    to_twin_half[4, 0].wait_recv()
     coef_half(4, 0)
     terms_half(4, 0)
     pass_on(4, 1)
@@ -429,14 +447,13 @@
         part_out[r, 3, half(1)] = (text_sum[at : at + HALF] + first_b[r].astype(F32)).astype(BF16)
         near_left[r, 1].start()
 
-    def row_total(r, c):
-        near_right[r, c].wait_recv()
-        near_left[r, c].wait_recv()
-        at = r * MINE + c * HALF
+    def row_total(r):
+        near_rows[r].wait_recv()
+        at = r * MINE
         return (
-            text_sum[at : at + HALF]
-            + second[r, 0, half(c)].astype(F32)
-            + second[r, 1, half(c)].astype(F32)
+            text_sum[at : at + ROWS]
+            + second[r, 0].astype(F32)
+            + second[r, 1].astype(F32)
         )
 
     def join_rows():
@@ -448,7 +465,7 @@
         rows = slice(c * HALF, (c + 1) * HALF)
         img_out[rows] = back_norm(img_ref[rows], inv_img[rows], grads[0, rows])
 
-    to_twin[4, 1].wait_recv()
+    to_twin_half[4, 1].wait_recv()
     coef_half(4, 1)
     terms_half(4, 1)
     text_row(1)
@@ -464,18 +481,23 @@
     far_b[0].start()
 
     def sum_row():
+        row_out[...] = row_total(1).astype(BF16)
         for c in range(2):
-            row_out[half(c)] = row_total(1, c).astype(BF16)
             over[c].start()
 
     def own_row():
-        for c in range(2):
-            text_sum[c * HALF : (c + 1) * HALF] = row_total(0, c)
+        text_sum[0:ROWS] = row_total(0)
 
     steps = (join_rows, functools.partial(join, 0), sum_row, own_row)
 
     usual = (1, 2, 3, 4)
-    moved = ({0: 0}, {0: 0, 1: 1}, {0: 1, 1: 2, 2: 2, ZS - 1: 4}, {0: 2, 1: 3, 2: 3, 3: 3})
+    high = range(ZS - HOPS, ZS)
+    moved = (
+        {0: 0} | dict.fromkeys(high, 2),
+        {0: 0, 1: 1} | dict.fromkeys(high, 3),
+        {0: 1, 1: 2, 2: 2} | dict.fromkeys(high, 4),
+        {0: 2, 1: 3, 2: 3, 3: 3},
+    )
 
     def at_place(place):
         for step, common, others in zip(steps, usual, moved):
@@ -500,30 +522,42 @@
     up_on((3, 3))
     climb(2, 2)
     climb(2, 3)
+    climb(1, 0)
     up_on((2, 1))
-    climb(1, 0)
     climb(1, 1)
     at_place(3)
+    up_on((2, 3))
     climb(1, 2)
     climb(1, 3)
-    up_on((2, 3), (1, 1))
     climb(0, 0)
     climb(0, 1)
     image_result(0)
-    up_on((1, 3))
     at_place(4)
-    for c in range(2):
-        over[c].wait_recv()
+    over_all.wait_recv()
     txt_out[...] = back_norm(txt_ref[...], inv_txt, text_sum[0:ROWS] + row_in[...].astype(F32))
     climb(0, 2)
     climb(0, 3)
     image_result(1)
 
-    for copy in copies:
-        copy.wait_send()
-
-
-N_COPIES = 3 * 8 + 10 + 2 + 4 + 4 + 2 + 2 + 10 + 2 * 16 + 2 + 2 + 4 + 4 + 2
+    def all_left(ref, leaves):
+        remote(ref, ref, twin, leaves, 0).wait_send()
+
+    all_left(imgs, TWIN)
+    all_left(txts, TEXT)
+    all_left(imgs.at[0:3], PART)
+    all_left(relay_down, DOWN)
+    all_left(chain_out, UP)
+
+    @pl.when(first_z)
+    def _():
+        all_left(relay_down, DOWN + 1)
+
+    @pl.when(last_z)
+    def _():
+        all_left(relay_up, UP + 1)
+
+
+N_ARRIVALS = 2 * 8 + 6 + 7 + 3 + (16 + 6) + 7
 
 
 def per_device(loops, images, texts, factor, shift):
@@ -557,9 +591,9 @@
             pltpu.SemaphoreType.DMA((2,)),
             pltpu.SemaphoreType.REGULAR,
             pltpu.VMEM((HOPS, ROWS, WIDE), BF16),
-            pltpu.VMEM((HOPS, ROWS, WIDE), BF16),
-            pltpu.SemaphoreType.DMA((N_COPIES,)),
-            pltpu.SemaphoreType.DMA((N_COPIES,)),
+            pltpu.VMEM((HOPS - 1, 2, SLICE, WIDE), BF16),
+            pltpu.SemaphoreType.DMA((N_LEAVES,)),
+            pltpu.SemaphoreType.DMA((N_ARRIVALS,)),
         ],
         compiler_params=pltpu.CompilerParams(
             collective_id=0, has_side_effects=True, vmem_limit_bytes=48 * 2**20

time: 66.2 us -> 64.8 us (0.979)
  Pallas kernels: 62.3 us -> 60.6 us
    pallas_call x1, Pallas kernels: 62.3 us -> 60.6 us  [per_device(): pl.pallas_call(functools.partial(kernel, loops), out_shape=(out, out), in...]
where the time goes in v4:
time: 64.8 us; the launch traced here: 64 us
  Pallas kernels  60.6 us (94%)
  between operations  1.93 us (3%)
  local copies, waits for them, and re-layouts  1.49 us (2%)
    pallas_call x1, Pallas kernels, per_device(): pl.pallas_call(functools.partial(kernel, loops), out_shape=(out, out), in...  60.6 us
    unnamed x2, local copies, waits for them, and re-layouts  1.49 us

profile of v4, /device:TPU:1, one launch (start us, length us, event | category | flops | bytes accessed | tf_op | source)
XLA Modules:
  0.0 64.0 jit_solution(3316320981944624548)
XLA Ops:
  1.9 60.6 %siglip.1 = (f32[64,1536]{1,0:T(8,128)S(1)}, f32[64,1536]{1,0:T(8,128)S(1)}) custom-call(f32[1]{0:T(128)S(6)} %copy.8.factor_ref, f32[1]{0:T(128)S(6)} %copy.9.shift_ref, bf16[64,1536]{1,0:T(8,128)(2,1)} %img_hbm.1, bf16[64,1536]{1,0:T(8,128)(2,1)} %txt_hbm.1), custom_call_target="tpu_custom_call" | custom-call | tf_op jit(solution)/shard_map/siglip/pallas_call | solution.py:568
  62.5 0.7 %copy.10 = f32[64,1536]{1,0:T(8,128)} copy(f32[64,1536]{1,0:T(8,128)S(1)} %get-tuple-element.4) | data formatting | bytes 786432
  63.2 0.7 %copy.11 = f32[64,1536]{1,0:T(8,128)} copy(f32[64,1536]{1,0:T(8,128)S(1)} %get-tuple-element.5) | data formatting | bytes 786432

commit v5 on v4

--- a/solution.py
+++ b/solution.py
@@ -50,8 +50,7 @@
     shift_ref,
     img_hbm,
     txt_hbm,
-    img_out,
-    txt_out,
+    both_out,
     img_ref,
     txt_ref,
     imgs,
@@ -230,7 +229,7 @@
             above,
             UP,
             last_z,
-            relay_up.at[h - 2, u // 2] if u % 2 and h > 1 else None,
+            relay_up.at[h - 3, u // 2] if u % 2 and h > 2 else None,
             far_above,
         )
         for h in range(1, HOPS + 1)
@@ -463,7 +462,7 @@
 
     def image_result(c):
         rows = slice(c * HALF, (c + 1) * HALF)
-        img_out[rows] = back_norm(img_ref[rows], inv_img[rows], grads[0, rows])
+        both_out[0, rows] = back_norm(img_ref[rows], inv_img[rows], grads[0, rows])
 
     to_twin_half[4, 1].wait_recv()
     coef_half(4, 1)
@@ -523,10 +522,8 @@
     climb(2, 2)
     climb(2, 3)
     climb(1, 0)
-    up_on((2, 1))
     climb(1, 1)
     at_place(3)
-    up_on((2, 3))
     climb(1, 2)
     climb(1, 3)
     climb(0, 0)
@@ -534,7 +531,7 @@
     image_result(0)
     at_place(4)
     over_all.wait_recv()
-    txt_out[...] = back_norm(txt_ref[...], inv_txt, text_sum[0:ROWS] + row_in[...].astype(F32))
+    both_out[1] = back_norm(txt_ref[...], inv_txt, text_sum[0:ROWS] + row_in[...].astype(F32))
     climb(0, 2)
     climb(0, 3)
     image_result(1)
@@ -557,19 +554,19 @@
         all_left(relay_up, UP + 1)
 
 
-N_ARRIVALS = 2 * 8 + 6 + 7 + 3 + (16 + 6) + 7
+N_ARRIVALS = 2 * 8 + 6 + 7 + 3 + (16 + 4) + 7
 
 
 def per_device(loops, images, texts, factor, shift):
     smem = pl.BlockSpec(memory_space=pltpu.SMEM)
     hbm = pl.BlockSpec(memory_space=pltpu.HBM)
     vmem = pl.BlockSpec(memory_space=pltpu.VMEM)
-    out = jax.ShapeDtypeStruct((ROWS, WIDE), F32)
-    return pl.pallas_call(
+    out = jax.ShapeDtypeStruct((2, ROWS, WIDE), F32)
+    both = pl.pallas_call(
         functools.partial(kernel, loops),
-        out_shape=(out, out),
+        out_shape=out,
         in_specs=[smem, smem, hbm, hbm],
-        out_specs=(vmem, vmem),
+        out_specs=vmem,
         scratch_shapes=[
             pltpu.VMEM((ROWS, WIDE), BF16),
             pltpu.VMEM((ROWS, WIDE), BF16),
@@ -591,7 +588,7 @@
             pltpu.SemaphoreType.DMA((2,)),
             pltpu.SemaphoreType.REGULAR,
             pltpu.VMEM((HOPS, ROWS, WIDE), BF16),
-            pltpu.VMEM((HOPS - 1, 2, SLICE, WIDE), BF16),
+            pltpu.VMEM((HOPS - 2, 2, SLICE, WIDE), BF16),
             pltpu.SemaphoreType.DMA((N_LEAVES,)),
             pltpu.SemaphoreType.DMA((N_ARRIVALS,)),
         ],
@@ -605,6 +602,7 @@
         pltpu.with_memory_space_constraint(images, pltpu.HBM),
         pltpu.with_memory_space_constraint(texts, pltpu.HBM),
     )
+    return both[0], both[1]
 
 
 def solution(mesh):

time: 64.8 us -> 63.6 us (0.981)
    unnamed x2 -> x0, local copies, waits for them, and re-layouts: 1.49 us -> none
    squeeze x0 -> x1, local copies, waits for them, and re-layouts: none -> 0.93 us  [per_device(): return (both[0], both[1])]
where the time goes in v5:
time: 63.6 us; the launch traced here: 63.4 us
  Pallas kernels  60.6 us (95%)
  between operations  1.93 us (3%)
  local copies, waits for them, and re-layouts  0.93 us (1%)
    pallas_call x1, Pallas kernels, per_device(): pl.pallas_call(functools.partial(kernel, loops), out_shape=out, in_specs=...  60.6 us

profile of v5, /device:TPU:1, one launch (start us, length us, event | category | flops | bytes accessed | tf_op | source)
XLA Modules:
  0.0 63.4 jit_solution(11570084408033754096)
XLA Ops:
  1.9 60.6 %siglip.1 = f32[2,64,1536]{2,1,0:T(8,128)S(1)} custom-call(f32[1]{0:T(128)S(6)} %copy.6.factor_ref, f32[1]{0:T(128)S(6)} %copy.7.shift_ref, bf16[64,1536]{1,0:T(8,128)(2,1)} %img_hbm.1, bf16[64,1536]{1,0:T(8,128)(2,1)} %txt_hbm.1), custom_call_target="tpu_custom_call" | custom-call | tf_op jit(solution)/shard_map/siglip/pallas_call | solution.py:565
  62.5 0.9 %slice_bitcast_fusion = (f32[64,1536]{1,0:T(8,128)}, f32[64,1536]{1,0:T(8,128)}) fusion(f32[2,64,1536]{2,1,0:T(8,128)S(1)} %siglip.1), kind=kLoop, calls=%fused_computation | loop fusion | bytes 1572864 | tf_op jit(solution)/shard_map/squeeze | solution.py:605

commit v6 on v5

--- a/solution.py
+++ b/solution.py
@@ -19,6 +19,7 @@
 WORDS = 2 * MINE
 DOWN, UP, TWIN, TEXT, PART = 0, 2, 4, 5, 6
 N_LEAVES = 7
+ROUND = ((4, 3), (3, 1), (3, 3), (2, 1))
 MESH = pl.DeviceIdType.MESH
 F32 = jnp.float32
 BF16 = jnp.bfloat16
@@ -160,17 +161,17 @@
             self.plain.wait_recv()
 
     down = {
-        (h, c): LoopLink(
-            imgs.at[h - 1, 0, half(c)],
-            imgs.at[h, 0, half(c)],
+        (h, u): LoopLink(
+            imgs.at[h - 1, 0, sliver(u)],
+            imgs.at[h, 0, sliver(u)],
             below,
             DOWN,
             first_z,
-            relay_down.at[h - 1, half(c)],
+            relay_down.at[h - 1, sliver(u)],
             far_below,
         )
         for h in range(1, HOPS + 1)
-        for c in range(2)
+        for u in range(SLICES)
     }
     to_twin = [link(imgs.at[0, 0], imgs.at[0, 1], twin, TWIN)]
     to_twin_half = {}
@@ -229,7 +230,7 @@
             above,
             UP,
             last_z,
-            relay_up.at[h - 3, u // 2] if u % 2 and h > 2 else None,
+            relay_up.at[ROUND.index((h, u))] if (h, u) in ROUND else None,
             far_above,
         )
         for h in range(1, HOPS + 1)
@@ -283,20 +284,23 @@
 
     for c in range(2):
         text_y[c].start()
-        pl.when(jnp.logical_not(first_z))(down[1, c].start)
+        for u in (2 * c, 2 * c + 1):
+            pl.when(jnp.logical_not(first_z))(down[1, u].start)
         text_right[0, c].start()
         text_left[0, c].start()
-    for c in range(2):
-        pl.when(first_z)(down[1, c].start)
+    for u in range(SLICES):
+        pl.when(first_z)(down[1, u].start)
     to_twin[0].start()
 
-    def pass_on(h, c):
-        down[h, c].wait_recv()
-        if h == 1:
-            pl.when(jnp.logical_not(first_z))(down[2, c].start)
-        elif h < HOPS:
-            down[h + 1, c].start()
-        to_twin_half[h, c].start()
+    def pass_on(h, *slivers):
+        for u in slivers:
+            down[h, u].wait_recv()
+            if h == 1:
+                pl.when(jnp.logical_not(first_z))(down[2, u].start)
+            elif h < HOPS:
+                down[h + 1, u].start()
+            if u % 2:
+                to_twin_half[h, u // 2].start()
 
     def send_on(links, at_edge, *keys):
         @pl.when(at_edge)
@@ -373,54 +377,61 @@
         else:
             grads[0, sliver(u)] = total
 
+    def far_text(side):
+        (text_right[1, 0] if side == 0 else text_left[1, 1]).wait_recv()
+        (text_far_a[1] if side == 0 else text_far_b[1]).start()
+
+    not_last = jnp.logical_not(last_z)
+    pl.when(not_last)(functools.partial(pass_on, 1, 0))
     spread_row(0)
-
-    pass_on(1, 0)
+    pl.when(last_z)(functools.partial(pass_on, 1, 0))
+    pass_on(1, 1, 2)
     spread_row(1)
     text_right[0, 0].wait_recv()
     text_far_a[0].start()
+    pass_on(1, 3)
     text_left[0, 1].wait_recv()
     text_far_b[0].start()
-    pass_on(1, 1)
 
     @pl.when(first_z)
     def _():
         down[2, 0].start()
+        down[2, 1].start()
         pl.semaphore_wait(go_sem, 1)
 
-    down_on((1, 0), (1, 1))
-    pl.when(first_z)(down[2, 1].start)
-
-    def far_text(side):
-        (text_right[1, 0] if side == 0 else text_left[1, 1]).wait_recv()
-        (text_far_a[1] if side == 0 else text_far_b[1]).start()
-
+    down_on((1, 0), (1, 1), (1, 2), (1, 3))
+    for u in (2, 3):
+        pl.when(first_z)(down[2, u].start)
     pl.when(last_z)(functools.partial(far_text, 0))
-    pass_on(2, 0)
-    pl.when(jnp.logical_not(last_z))(functools.partial(far_text, 0))
+    pass_on(2, 0, 1)
+    pl.when(not_last)(functools.partial(far_text, 0))
     pl.when(last_z)(functools.partial(far_text, 1))
-    pass_on(2, 1)
-    pl.when(jnp.logical_not(last_z))(functools.partial(far_text, 1))
-
+    pass_on(2, 2, 3)
+    pl.when(not_last)(functools.partial(far_text, 1))
     down_on((2, 0), (2, 1))
     pass_on(3, 0)
+    down_on((2, 2), (2, 3))
+    pass_on(3, 1)
     down_on((3, 0))
-    pass_on(3, 1)
+    pass_on(3, 2)
     down_on((3, 1))
+    pass_on(3, 3)
+    down_on((3, 2))
     text_rest.wait_recv()
+    down_on((3, 3))
     for h in range(2):
         from_twin(h)
     coef_hops(0, 2)
-    pass_on(4, 0)
-    down_on((4, 0))
+    pass_on(4, 0, 1)
+    down_on((4, 0), (4, 1))
     for h in range(2, 4):
         from_twin(h)
     coef_hops(2, 4)
-    down_on((4, 1))
+    down_on((4, 2), (4, 3))
     to_twin_half[4, 0].wait_recv()
     coef_half(4, 0)
     terms_half(4, 0)
-    pass_on(4, 1)
+    pass_on(4, 2, 3)
     terms_hops(0, 4)
     climb(4, 0)
     climb(4, 1)
@@ -472,7 +483,6 @@
     far_b[1].start()
     near_right[1, 1].start()
     near_left[1, 0].start()
-    up_on((4, 1))
     climb(4, 2)
     climb(4, 3)
     text_row(0)
@@ -522,10 +532,11 @@
     climb(2, 2)
     climb(2, 3)
     climb(1, 0)
-    climb(1, 1)
+    up_on((2, 1))
     at_place(3)
     climb(1, 2)
     climb(1, 3)
+    climb(1, 1)
     climb(0, 0)
     climb(0, 1)
     image_result(0)
@@ -554,7 +565,7 @@
         all_left(relay_up, UP + 1)
 
 
-N_ARRIVALS = 2 * 8 + 6 + 7 + 3 + (16 + 4) + 7
+N_ARRIVALS = 2 * 16 + 6 + 7 + 3 + (16 + 4) + 7
 
 
 def per_device(loops, images, texts, factor, shift):
@@ -588,7 +599,7 @@
             pltpu.SemaphoreType.DMA((2,)),
             pltpu.SemaphoreType.REGULAR,
             pltpu.VMEM((HOPS, ROWS, WIDE), BF16),
-            pltpu.VMEM((HOPS - 2, 2, SLICE, WIDE), BF16),
+            pltpu.VMEM((len(ROUND), SLICE, WIDE), BF16),
             pltpu.SemaphoreType.DMA((N_LEAVES,)),
             pltpu.SemaphoreType.DMA((N_ARRIVALS,)),
         ],

time: 63.6 us -> 63.1 us (level); the launches traced: 63.4 us -> 62 us
  Pallas kernels: 60.6 us -> 59.2 us
    pallas_call x1, Pallas kernels: 60.6 us -> 59.2 us  [per_device(): pl.pallas_call(functools.partial(kernel, loops), out_shape=out, in_specs=...]
where the time goes in v6:
time: 63.1 us; the launch traced here: 62 us
  Pallas kernels  59.2 us (94%)
  between operations  1.93 us (3%)
  local copies, waits for them, and re-layouts  0.93 us (1%)
    pallas_call x1, Pallas kernels, per_device(): pl.pallas_call(functools.partial(kernel, loops), out_shape=out, in_specs=...  59.2 us

profile of v6, /device:TPU:1, one launch (start us, length us, event | category | flops | bytes accessed | tf_op | source)
XLA Modules:
  0.0 62.0 jit_solution(10298788023632403080)
XLA Ops:
  1.9 59.2 %siglip.1 = f32[2,64,1536]{2,1,0:T(8,128)S(1)} custom-call(f32[1]{0:T(128)S(6)} %copy.6.factor_ref, f32[1]{0:T(128)S(6)} %copy.7.shift_ref, bf16[64,1536]{1,0:T(8,128)(2,1)} %img_hbm.1, bf16[64,1536]{1,0:T(8,128)(2,1)} %txt_hbm.1), custom_call_target="tpu_custom_call" | custom-call | tf_op jit(solution)/shard_map/siglip/pallas_call | solution.py:576
  61.1 0.9 %slice_bitcast_fusion = (f32[64,1536]{1,0:T(8,128)}, f32[64,1536]{1,0:T(8,128)}) fusion(f32[2,64,1536]{2,1,0:T(8,128)S(1)} %siglip.1), kind=kLoop, calls=%fused_computation | loop fusion | bytes 1572864 | tf_op jit(solution)/shard_map/squeeze | solution.py:616

commit v7 on v6

--- a/solution.py
+++ b/solution.py
@@ -538,14 +538,14 @@
     climb(1, 3)
     climb(1, 1)
     climb(0, 0)
-    climb(0, 1)
-    image_result(0)
+    climb(0, 2)
+    climb(0, 3)
+    image_result(1)
     at_place(4)
     over_all.wait_recv()
     both_out[1] = back_norm(txt_ref[...], inv_txt, text_sum[0:ROWS] + row_in[...].astype(F32))
-    climb(0, 2)
-    climb(0, 3)
-    image_result(1)
+    climb(0, 1)
+    image_result(0)
 
     def all_left(ref, leaves):
         remote(ref, ref, twin, leaves, 0).wait_send()

time: 63.1 us -> 62.8 us (level)
  no operation moved by 1% of the time
where the time goes in v7:
time: 62.8 us; the launch traced here: 61.7 us
  Pallas kernels  58.9 us (94%)
  between operations  1.93 us (3%)
  local copies, waits for them, and re-layouts  0.93 us (1%)
    pallas_call x1, Pallas kernels, per_device(): pl.pallas_call(functools.partial(kernel, loops), out_shape=out, in_specs=...  58.9 us

profile of v7, /device:TPU:1, one launch (start us, length us, event | category | flops | bytes accessed | tf_op | source)
XLA Modules:
  0.0 61.7 jit_solution(698078272292038764)
XLA Ops:
  1.9 58.9 %siglip.1 = f32[2,64,1536]{2,1,0:T(8,128)S(1)} custom-call(f32[1]{0:T(128)S(6)} %copy.6.factor_ref, f32[1]{0:T(128)S(6)} %copy.7.shift_ref, bf16[64,1536]{1,0:T(8,128)(2,1)} %img_hbm.1, bf16[64,1536]{1,0:T(8,128)(2,1)} %txt_hbm.1), custom_call_target="tpu_custom_call" | custom-call | tf_op jit(solution)/shard_map/siglip/pallas_call | solution.py:576
  60.8 0.9 %slice_bitcast_fusion = (f32[64,1536]{1,0:T(8,128)}, f32[64,1536]{1,0:T(8,128)}) fusion(f32[2,64,1536]{2,1,0:T(8,128)S(1)} %siglip.1), kind=kLoop, calls=%fused_computation | loop fusion | bytes 1572864 | tf_op jit(solution)/shard_map/squeeze | solution.py:616

commit v8 on v7

--- a/solution.py
+++ b/solution.py
@@ -424,17 +424,25 @@
     coef_hops(0, 2)
     pass_on(4, 0, 1)
     down_on((4, 0), (4, 1))
-    for h in range(2, 4):
-        from_twin(h)
-    coef_hops(2, 4)
+    def later_hops():
+        for h in range(2, 4):
+            from_twin(h)
+        coef_hops(2, 4)
+
+    def first_climbs():
+        climb(4, 0)
+        climb(4, 1)
+
+    pl.when(not_last)(later_hops)
     down_on((4, 2), (4, 3))
     to_twin_half[4, 0].wait_recv()
     coef_half(4, 0)
     terms_half(4, 0)
+    pl.when(last_z)(later_hops)
+    pl.when(last_z)(first_climbs)
     pass_on(4, 2, 3)
     terms_hops(0, 4)
-    climb(4, 0)
-    climb(4, 1)
+    pl.when(not_last)(first_climbs)
 
     def text_row(r):
         at = r * MINE

time: 62.8 us -> 63.9 us (1.018); the launches traced: 61.7 us -> 63.8 us
  Pallas kernels: 58.9 us -> 60.9 us
    pallas_call x1, Pallas kernels: 58.9 us -> 60.9 us  [per_device(): pl.pallas_call(functools.partial(kernel, loops), out_shape=out, in_specs=...]
where the time goes in v8:
time: 63.9 us; the launch traced here: 63.8 us
  Pallas kernels  60.9 us (95%)
  between operations  1.93 us (3%)
  local copies, waits for them, and re-layouts  0.93 us (1%)
    pallas_call x1, Pallas kernels, per_device(): pl.pallas_call(functools.partial(kernel, loops), out_shape=out, in_specs=...  60.9 us

profile of v8, /device:TPU:1, one launch (start us, length us, event | category | flops | bytes accessed | tf_op | source)
XLA Modules:
  0.0 63.8 jit_solution(6195364606728260875)
XLA Ops:
  1.9 60.9 %siglip.1 = f32[2,64,1536]{2,1,0:T(8,128)S(1)} custom-call(f32[1]{0:T(128)S(6)} %copy.6.factor_ref, f32[1]{0:T(128)S(6)} %copy.7.shift_ref, bf16[64,1536]{1,0:T(8,128)(2,1)} %img_hbm.1, bf16[64,1536]{1,0:T(8,128)(2,1)} %txt_hbm.1), custom_call_target="tpu_custom_call" | custom-call | tf_op jit(solution)/shard_map/siglip/pallas_call | solution.py:584
  62.9 0.9 %slice_bitcast_fusion = (f32[64,1536]{1,0:T(8,128)}, f32[64,1536]{1,0:T(8,128)}) fusion(f32[2,64,1536]{2,1,0:T(8,128)S(1)} %siglip.1), kind=kLoop, calls=%fused_computation | loop fusion | bytes 1572864 | tf_op jit(solution)/shard_map/squeeze | solution.py:624
